TPU v7x, 128 devices: a whole 4x4x4 slice. The times are simulated.
128 devices in a mesh: phase: 2 (over core), dp: 16 (over y, x), mp: 4 (over z).
Axes of the slice: x: 4, y: 4, z: 4, core: 2. Of those that a mesh axis runs over, the one named last changes fastest.
Arguments:
- queries: bfloat16 [16384, 2048], P(('phase', 'dp'), 'mp'), may hold values from -150 to 150
- grad_out: bfloat16 [16384, 2048], P(('phase', 'dp'), 'mp'), may hold values from -6 to 6
- encoded: bfloat16 [256, 128, 4096], P(('phase', 'dp'), None, 'mp'), may hold values from -6 to 6
- key_weight: bfloat16 [4096, 2048], P(None, 'mp'), may hold values from -0.09375 to 0.09375
- value_weight: bfloat16 [4096, 2048], P(None, 'mp'), may hold values from -0.09375 to 0.09375
- send_rows: int32 [32, 32, 1], P(('phase', 'dp')), may hold values from 0 to 7, as said below
- read_slots: int32 [256, 2], P(('phase', 'dp')), may hold values from 0 to 31, as said below
Outputs:
- attended: bfloat16 [16384, 2048], P(('phase', 'dp'), 'mp')
- grad_q: bfloat16 [16384, 2048], P(('phase', 'dp'), 'mp')
- grad_e: bfloat16 [256, 128, 4096], P(('phase', 'dp'), None, 'mp')
Inputs may be any that keep to these rules, and one draw needn't show every extreme that they name: send_rows[o, r, c] is a local row (below 8) of owner o's neighbours; one row may be sent to several readers and in several slots; slots that no span of reader r reads hold 0. `read_slots`: all 16 entries of one reader's spans name different slots; every reader fills all 1 slots of at least one owner.
All inputs are finite; a program needn't handle non-finite values.
Results may differ from a plain program's by a relative error of at most 0.013.
Values may be sent and summed in bfloat16 or wider, within the bound.
A program may use at most 128 MiB of HBM per device.

v0:
```python
import jax
import jax.numpy as jnp
from jax import lax
from jax.sharding import PartitionSpec as P

HS = 128
CLEN = 64
NLEN = 128


def attend_blocks(query_blocks, key_blocks, value_blocks, scaling):
    scores = (
        jnp.einsum("sqhd,skhd->shqk", query_blocks, key_blocks, preferred_element_type=jnp.float32)
        * scaling
    )
    peaks = jnp.max(scores, -1)
    weights = jnp.exp(scores - peaks[..., None])
    totals = jnp.sum(weights, -1)
    partial_out = jnp.einsum(
        "shqk,skhd->sqhd",
        weights.astype(jnp.bfloat16),
        value_blocks,
        preferred_element_type=jnp.float32,
    )
    return (partial_out, peaks, totals)


def attend_grads(
    query_blocks, key_blocks, value_blocks, grad_blocks, log_totals, correction, scaling
):
    scores = (
        jnp.einsum("sqhd,skhd->shqk", query_blocks, key_blocks, preferred_element_type=jnp.float32)
        * scaling
    )
    row_probs = jnp.exp(scores - log_totals[..., None])
    grad_v = jnp.einsum(
        "shqk,sqhd->skhd",
        row_probs.astype(jnp.bfloat16),
        grad_blocks,
        preferred_element_type=jnp.float32,
    ).astype(jnp.bfloat16)
    grad_p = jnp.einsum(
        "sqhd,skhd->shqk", grad_blocks, value_blocks, preferred_element_type=jnp.float32
    )
    grad_s = (row_probs * (grad_p - correction[..., None])).astype(jnp.bfloat16)
    grad_query = (
        jnp.einsum("shqk,skhd->sqhd", grad_s, key_blocks, preferred_element_type=jnp.float32)
        * scaling
    )
    grad_k = (
        jnp.einsum("shqk,sqhd->skhd", grad_s, query_blocks, preferred_element_type=jnp.float32)
        * scaling
    ).astype(jnp.bfloat16)
    return (grad_query, grad_k, grad_v)


def body(queries, grad_out, encoded, key_weight, value_weight, send_rows, read_slots):
    scaling = HS ** (-0.5)
    groups = lax.axis_size(("phase", "dp"))
    capacity = send_rows.shape[2]
    slot_count = groups * capacity
    local_count = encoded.shape[0]
    heads_here = key_weight.shape[1] // HS
    span_count = read_slots.shape[0]
    rows_flat = encoded.reshape(local_count * NLEN, encoded.shape[2])
    pieces = lax.all_gather(rows_flat, "mp", axis=1, tiled=True)
    key_row_list = key_weight
    value_rows = value_weight
    key_acc = jnp.dot(pieces, key_row_list, preferred_element_type=jnp.float32)
    value_acc = jnp.dot(pieces, value_rows, preferred_element_type=jnp.float32)
    keys_local = key_acc.astype(jnp.bfloat16).reshape(local_count, NLEN, heads_here * HS)
    values_local = value_acc.astype(jnp.bfloat16).reshape(local_count, NLEN, heads_here * HS)
    picked_rows = send_rows.reshape(slot_count)
    owner_hits = (picked_rows[None, :] == jnp.arange(local_count, dtype=jnp.int32)[:, None]).astype(
        jnp.bfloat16
    )
    flat_reads = read_slots.reshape(2 * span_count)
    matches = flat_reads[None, :] == jnp.arange(slot_count, dtype=jnp.int32)[:, None]
    live_slot = jnp.any(matches, 1)
    source_read = jnp.sum(
        jnp.where(matches, jnp.arange(2 * span_count, dtype=jnp.int32)[None, :], 0), 1
    )
    source_span = source_read // 2

    def to_slots(per_span):
        gathered_rows = jnp.take(per_span, source_span, axis=0)
        keep_mask = live_slot.reshape((slot_count,) + (1,) * (per_span.ndim - 1))
        return jnp.where(keep_mask, gathered_rows, jnp.zeros_like(gathered_rows))

    query_spans = queries.reshape(span_count, CLEN, heads_here, HS)
    grad_spans = grad_out.reshape(span_count, CLEN, heads_here, HS)
    query_slots = to_slots(query_spans)
    grad_slots = to_slots(grad_spans)
    outgoing = (
        jnp.take(keys_local, picked_rows, axis=0).reshape(groups, capacity, NLEN, heads_here * HS),
        jnp.take(values_local, picked_rows, axis=0).reshape(
            groups, capacity, NLEN, heads_here * HS
        ),
    )
    fetched_keys, fetched_values = (
        lax.all_to_all(outgoing[0], ("phase", "dp"), split_axis=0, concat_axis=0, tiled=True),
        lax.all_to_all(outgoing[1], ("phase", "dp"), split_axis=0, concat_axis=0, tiled=True),
    )
    key_slots = fetched_keys.reshape(slot_count, NLEN, heads_here, HS)
    value_slots = fetched_values.reshape(slot_count, NLEN, heads_here, HS)
    partial_out, peaks, totals = attend_blocks(query_slots, key_slots, value_slots, scaling)
    chosen = jnp.take(partial_out, read_slots, axis=0)
    chosen_peaks = jnp.take(peaks, read_slots, axis=0)
    chosen_totals = jnp.take(totals, read_slots, axis=0)
    overall = jnp.max(chosen_peaks, 1)
    factors = jnp.exp(chosen_peaks - overall[:, None])
    denominator = jnp.sum(factors * chosen_totals, 1)
    blended = (
        jnp.sum(jnp.swapaxes(factors, 2, 3)[..., None] * chosen, 1)
        / jnp.swapaxes(denominator, 1, 2)[..., None]
    )
    attended_here = blended.astype(jnp.bfloat16).reshape(queries.shape)
    log_totals = overall + jnp.log(denominator)
    correction = jnp.swapaxes(jnp.sum(grad_spans.astype(jnp.float32) * blended, -1), 1, 2)
    attended, log_totals, correction = (attended_here, log_totals, correction)
    grad_q_slots, grad_k_slots, grad_v_slots = attend_grads(
        query_slots,
        key_slots,
        value_slots,
        grad_slots,
        to_slots(log_totals),
        to_slots(correction),
        scaling,
    )
    back_keys, back_values = (
        lax.all_to_all(
            grad_k_slots.reshape(groups, capacity, NLEN, heads_here * HS),
            ("phase", "dp"),
            split_axis=0,
            concat_axis=0,
            tiled=True,
        ),
        lax.all_to_all(
            grad_v_slots.reshape(groups, capacity, NLEN, heads_here * HS),
            ("phase", "dp"),
            split_axis=0,
            concat_axis=0,
            tiled=True,
        ),
    )
    grad_k_flat = back_keys.reshape(slot_count, NLEN * heads_here * HS)
    grad_v_flat = back_values.reshape(slot_count, NLEN * heads_here * HS)
    grad_q = (
        jnp.sum(jnp.take(grad_q_slots, read_slots, axis=0), 1)
        .astype(jnp.bfloat16)
        .reshape(queries.shape)
    )
    grad_k_rows = (
        jnp.dot(owner_hits, grad_k_flat, preferred_element_type=jnp.float32)
        .astype(jnp.bfloat16)
        .reshape(local_count * NLEN, heads_here * HS)
    )
    grad_v_rows = (
        jnp.dot(owner_hits, grad_v_flat, preferred_element_type=jnp.float32)
        .astype(jnp.bfloat16)
        .reshape(local_count * NLEN, heads_here * HS)
    )
    contract = (((1,), (1,)), ((), ()))
    key_row_list = key_weight
    value_rows = value_weight
    grad_features = lax.psum_scatter(
        lax.dot_general(key_row_list, grad_k_rows, contract, preferred_element_type=jnp.float32)
        + lax.dot_general(value_rows, grad_v_rows, contract, preferred_element_type=jnp.float32),
        "mp",
        scatter_dimension=0,
        tiled=True,
    )
    grad_e = (
        jnp.transpose(grad_features)
        .reshape(local_count, NLEN, encoded.shape[2])
        .astype(jnp.bfloat16)
    )
    return (attended, grad_q, grad_e)


def solution(mesh):
    return jax.shard_map(
        body,
        mesh=mesh,
        in_specs=(
            P(("phase", "dp"), "mp"),
            P(("phase", "dp"), "mp"),
            P(("phase", "dp"), None, "mp"),
            P(None, "mp"),
            P(None, "mp"),
            P(("phase", "dp"), None, None),
            P(("phase", "dp"), None),
        ),
        out_specs=(
            P(("phase", "dp"), "mp"),
            P(("phase", "dp"), "mp"),
            P(("phase", "dp"), None, "mp"),
        ),
        check_vma=False,
    )
```

profile of v0, /device:TPU:16, one launch (start us, length us, event | category | flops | bytes accessed | tf_op | source)
XLA Modules:
  0.0 589.8 jit_solution(7982972810169973517)
XLA Ops:
  9.2 86.0 %all-gather.2.cloned.1.call-done = bf16[1024,4096]{1,0:T(8,128)(2,1)} async-done(((bf16[1024,1024]{1,0:T(8,128)(2,1)}), bf16[1024,4096]{1,0:T(8,128)(2,1)}) %all-gather.2.cloned.1.call-update) | async-done | bytes 8388624 | tf_op jit(solution)/shard_map/all_gather | solution.py:66
  95.2 9.0 %convolution_convert_fusion.3 = bf16[1024,512]{1,0:T(8,128)(2,1)S(1)} fusion(bf16[1024,4096]{1,0:T(8,128)(2,1)} %all-gather.2.cloned.1.call-done, bf16[4096,512]{1,0:T(8,128)(2,1)} %param.21), kind=kOutput, calls=%fused_computation.35 | convolution fusion | flops 4295491584 | bytes 13631488 | tf_op jit(solution)/shard_map/dot_general | solution.py:70
  104.3 2.8 gather_fusion.3
  107.0 9.0 %convolution_convert_fusion.4 = bf16[1024,512]{1,0:T(8,128)(2,1)S(1)} fusion(bf16[1024,4096]{1,0:T(8,128)(2,1)} %all-gather.2.cloned.1.call-done, bf16[4096,512]{1,0:T(8,128)(2,1)} %param.20), kind=kOutput, calls=%fused_computation.36 | convolution fusion | flops 4295491584 | bytes 13631488 | tf_op jit(solution)/shard_map/dot_general | solution.py:69
  116.1 2.7 gather_fusion.1
  118.8 5.2 select_bitcast_fusion
  124.1 56.6 %all_to_all.20 = bf16[32,1,128,512]{3,2,1,0:T(8,128)(2,1)} all-to-all(bf16[32,1,128,512]{3,2,1,0:T(8,128)(2,1)S(1)} %get-tuple-element.17), channel_id=1, replica_groups=mesh['phase'=2,'dp'=16,'mp'=4] {'phase','dp'}, dimensions={0} | all-to-all | bytes 8388608 | tf_op jit(solution)/shard_map/all_to_all | solution.py:101
  180.6 7.4 %all-to-all-start.1 = ((bf16[32,1,128,512]{3,2,1,0:T(8,128)(2,1)}), bf16[32,1,128,512]{3,2,1,0:T(8,128)(2,1)}, u32[]{:S(2)}, u32[]{:S(2)}) async-start(bf16[32,1,128,512]{3,2,1,0:T(8,128)(2,1)} %get-tuple-element.16), calls=%async_computation.1 | async-start | bytes 8388608 | tf_op jit(solution)/shard_map/all_to_all | solution.py:102
  193.0 6.4 %copy.110 = bf16[32,1,128,512]{2,3,0,1:T(8,128)(2,1)} copy(bf16[32,1,128,512]{3,2,1,0:T(8,128)(2,1)} %all_to_all.20) | data formatting | bytes 8388608 | tf_op jit(solution)/shard_map/all_to_all | solution.py:101
  199.4 5.5 multiply_reduce_fusion
  205.5 4.0 fusion
  210.9 33.3 %all-to-all-done.1 = bf16[32,1,128,512]{3,2,1,0:T(8,128)(2,1)} async-done(((bf16[32,1,128,512]{3,2,1,0:T(8,128)(2,1)}), bf16[32,1,128,512]{3,2,1,0:T(8,128)(2,1)}, u32[]{:S(2)}, u32[]{:S(2)}) %all-to-all-start.1) | async-done | bytes 4194336 | tf_op jit(solution)/shard_map/all_to_all | solution.py:102
  244.1 6.4 %copy.115 = bf16[32,1,128,512]{2,3,0,1:T(8,128)(2,1)} copy(bf16[32,1,128,512]{3,2,1,0:T(8,128)(2,1)} %all-to-all-done.1) | data formatting | bytes 8388608 | tf_op jit(solution)/shard_map/all_to_all | solution.py:102
  250.6 9.0 %convolution_bitcast_fusion = f32[32,64,4,128]{3,1,2,0:T(8,128)} fusion(bf16[32,128,4,128]{1,3,2,0:T(8,128)(2,1)} %bitcast.84, f32[32,4,64,128]{3,2,1,0:T(8,128)} %get-tuple-element.19, f32[32,4,64]{2,1,0:T(4,128)S(1)} %get-tuple-element.18), kind=kOutput, calls=%fused_computation.25 | convolution fusion | flops 271581184 | bytes 12615680 | tf_op jit(solution)/shard_map/shqk,skhd->sqhd/dot_general | solution.py:19
  259.5 2.9 gather_fusion.4
  264.7 5.5 multiply_convert_fusion.1
  270.3 3.6 multiply_convert_fusion
  273.9 6.5 %copy.130 = bf16[32,1,128,512]{3,2,1,0:T(8,128)(2,1)} copy(bf16[32,1,128,512]{2,3,0,1:T(8,128)(2,1)} %bitcast.91) | data formatting | bytes 8388608 | tf_op jit(solution)/shard_map/reshape | solution.py:132
  280.4 5.5 all-to-all-start.2
  286.0 5.8 convolution_convert_fusion.2
  291.8 6.5 %copy.131 = bf16[32,1,128,512]{3,2,1,0:T(8,128)(2,1)} copy(bf16[32,1,128,512]{2,3,0,1:T(8,128)(2,1)} %bitcast.86) | data formatting | bytes 8388608 | tf_op jit(solution)/shard_map/reshape | solution.py:139
  298.3 42.9 %all-to-all-done.2 = bf16[32,1,128,512]{3,2,1,0:T(8,128)(2,1)} async-done(((bf16[32,1,128,512]{3,2,1,0:T(8,128)(2,1)}), bf16[32,1,128,512]{3,2,1,0:T(8,128)(2,1)}, u32[]{:S(2)}, u32[]{:S(2)}) %all-to-all-start.2) | async-done | bytes 4194336 | tf_op jit(solution)/shard_map/all_to_all | solution.py:131
  341.1 5.0 all-to-all-start.3
  346.2 4.6 copy.139
  352.9 48.6 %all-to-all-done.3 = bf16[32,1,128,512]{3,2,1,0:T(8,128)(2,1)} async-done(((bf16[32,1,128,512]{3,2,1,0:T(8,128)(2,1)}), bf16[32,1,128,512]{3,2,1,0:T(8,128)(2,1)}, u32[]{:S(2)}, u32[]{:S(2)}) %all-to-all-start.3) | async-done | bytes 4194336 | tf_op jit(solution)/shard_map/all_to_all | solution.py:138
  401.5 4.6 copy.140
  407.2 12.9 %fusion.19 = f32[1024,4096]{1,0:T(8,128)} fusion(bf16[1024,512]{1,0:T(8,128)(2,1)} %reshape.115, bf16[4096,512]{1,0:T(8,128)(2,1)} %param.20), kind=kOutput, calls=%fused_computation.72 | convolution fusion | flops 4294967296 | bytes 22020096 | tf_op jit(solution)/shard_map/dot_general | solution.py:167
  420.2 11.8 %add_bitcast_fusion = f32[4096,1024]{0,1:T(8,128)} fusion(f32[1024,4096]{1,0:T(8,128)} %fusion.19, bf16[1024,512]{1,0:T(8,128)(2,1)S(1)} %reshape.118, bf16[4096,512]{1,0:T(8,128)(2,1)S(1)} %copy-done.5), kind=kOutput, calls=%fused_computation.12 | convolution fusion | flops 4299161600 | bytes 38797312 | tf_op jit(solution)/shard_map/dot_general | solution.py:168
  433.6 7.2 %multiply_bitcast_fusion = f32[32,64,4,128]{3,1,2,0:T(8,128)} fusion(bf16[32,128,4,128]{1,3,2,0:T(8,128)(2,1)} %bitcast.83, bf16[32,4,64,128]{3,2,1,0:T(8,128)(2,1)S(1)} %copy-done.7), kind=kOutput, calls=%fused_computation.16 | convolution fusion | flops 269484032 | bytes 10485760 | tf_op jit(solution)/shard_map/shqk,skhd->sqhd/dot_general | solution.py:47
  440.8 2.9 gather_fusion.9
  445.9 132.8 %reduce-scatter.2.cloned.1.call-done = f32[1024,1024]{0,1:T(8,128)} async-done(((f32[4096,1024]{0,1:T(8,128)}), f32[1024,1024]{0,1:T(8,128)}) %reduce-scatter.2.cloned.1.call-update) | async-done | bytes 4194320 | tf_op jit(solution)/shard_map/reduce_scatter | solution.py:166
  578.7 3.8 convert_element_type.76
  (67 shorter events, 18.3 us)
Async XLA Ops:
  7.2 88.0 %all-gather.2.cloned.1.call-start = ((), (), s32[]{:S(2)}) async-start(), calls=%async_computation.5 | async-start | bytes 10485760 | tf_op jit(solution)/shard_map/all_gather | solution.py:66
  180.6 7.4 %copy-start.10 = (s32[8,2]{0,1:T(2,128)S(1)}, s32[8,2]{0,1:T(2,128)}, u32[]{:S(2)}) copy-start(s32[8,2]{0,1:T(2,128)} %param.23) | copy-start | bytes 196
  180.6 7.8 %copy-start.8 = (bf16[512,512]{1,0:T(8,128)(2,1)S(1)}, bf16[512,512]{1,0:T(8,128)(2,1)}, u32[]{:S(2)}) copy-start(bf16[512,512]{1,0:T(8,128)(2,1)} %param.18) | copy-start | bytes 1572868
  180.6 8.8 %copy-start.9 = (bf16[512,512]{1,0:T(8,128)(2,1)S(1)}, bf16[512,512]{1,0:T(8,128)(2,1)}, u32[]{:S(2)}) copy-start(bf16[512,512]{1,0:T(8,128)(2,1)} %param.17) | copy-start | bytes 1572868
  180.6 63.5 %all-to-all-start.1 = ((bf16[32,1,128,512]{3,2,1,0:T(8,128)(2,1)}), bf16[32,1,128,512]{3,2,1,0:T(8,128)(2,1)}, u32[]{:S(2)}, u32[]{:S(2)}) async-start(bf16[32,1,128,512]{3,2,1,0:T(8,128)(2,1)} %get-tuple-element.16), calls=%async_computation.1 | async-start | bytes 8388608 | tf_op jit(solution)/shard_map/all_to_all | solution.py:102
  188.6 0.8 copy-start.3
  190.7 8.7 %copy-start.1 = (bf16[32,64,4,128]{3,1,2,0:T(8,128)(2,1)}, bf16[32,64,4,128]{3,1,2,0:T(8,128)(2,1)S(1)}, u32[]{:S(2)}) copy-start(bf16[32,64,4,128]{3,1,2,0:T(8,128)(2,1)S(1)} %gather_fusion) | copy-start | bytes 6291460
  259.5 3.7 copy-start.4
  264.7 5.5 copy-start.2
  270.2 3.6 copy-start.6
  280.4 5.6 copy-start
  280.4 60.7 %all-to-all-start.2 = ((bf16[32,1,128,512]{3,2,1,0:T(8,128)(2,1)}), bf16[32,1,128,512]{3,2,1,0:T(8,128)(2,1)}, u32[]{:S(2)}, u32[]{:S(2)}) async-start(bf16[32,1,128,512]{3,2,1,0:T(8,128)(2,1)} %copy.130), calls=%async_computation.2 | async-start | bytes 8388608 | tf_op jit(solution)/shard_map/all_to_all | solution.py:131
  341.1 60.4 %all-to-all-start.3 = ((bf16[32,1,128,512]{3,2,1,0:T(8,128)(2,1)}), bf16[32,1,128,512]{3,2,1,0:T(8,128)(2,1)}, u32[]{:S(2)}, u32[]{:S(2)}) async-start(bf16[32,1,128,512]{3,2,1,0:T(8,128)(2,1)} %copy.131), calls=%async_computation.3 | async-start | bytes 8388608 | tf_op jit(solution)/shard_map/all_to_all | solution.py:138
  346.2 232.5 %reduce-scatter.2.cloned.1.call-start = ((), (), s32[]{:S(2)}) async-start(), calls=%async_computation.6 | async-start | bytes 20971520 | tf_op jit(solution)/shard_map/reduce_scatter | solution.py:166
  346.2 4.6 copy-start.11
  407.2 12.9 %copy-start.5 = (bf16[4096,512]{1,0:T(8,128)(2,1)S(1)}, bf16[4096,512]{1,0:T(8,128)(2,1)}, u32[]{:S(2)}) copy-start(bf16[4096,512]{1,0:T(8,128)(2,1)} %param.21) | copy-start | bytes 12582916
  432.0 1.6 copy-start.7
Sparse Core Ops, SparseCore 0:
  9.7 85.5 all-gather.1
  432.1 146.5 reduce-scatter.1
where the time goes:
time: 598 us; the launch traced here: 590 us
  waiting for transfers between devices  344 us (58%)
  matrix products  80.7 us (13%)
  local copies, waits for them, and re-layouts  58.8 us (10%)
  blocking collectives  56.6 us (9%)
  starting transfers between devices  18 us (3%)
  other arithmetic  16.7 us (3%)
  between operations  14.8 us (2%)
    reduce_scatter x1, waiting for transfers between devices, body(): lax.psum_scatter(lax.dot_general(key_row_list, grad_k_rows, contract, pre...  133 us
    all_gather x1, waiting for transfers between devices, body(): pieces = lax.all_gather(rows_flat, 'mp', axis=1, tiled=True)  86 us
    all_to_all x1, blocking collectives, body(): lax.all_to_all(outgoing[0], ('phase', 'dp'), split_axis=0, concat_axis=0,...  56.6 us
    all_to_all x1, waiting for transfers between devices, body(): lax.all_to_all(grad_v_slots.reshape(groups, capacity, NLEN, heads_here *...  48.6 us
    all_to_all x1, waiting for transfers between devices, body(): lax.all_to_all(grad_k_slots.reshape(groups, capacity, NLEN, heads_here *...  42.9 us
    all_to_all x1, waiting for transfers between devices, body(): lax.all_to_all(outgoing[1], ('phase', 'dp'), split_axis=0, concat_axis=0,...  33.3 us
    dot_general x1, matrix products, body(): lax.dot_general(key_row_list, grad_k_rows, contract, preferred_element_ty...  12.9 us
  transfers between devices with their start and end apart: 5, of which 5 were waited for; matrix products, arithmetic and copies ran while one was open for 9% of the time, Pallas kernels for 0%

commit v1 on v0

v1 whole, which is shorter than its diff:
```python
import functools

import jax
import jax.numpy as jnp
from jax import lax
from jax.experimental import pallas as pl
from jax.experimental.pallas import tpu as pltpu
from jax.sharding import PartitionSpec as P

HS = 128
CLEN = 64
NLEN = 128
SCALE = HS ** (-0.5)
LAST = (((1,), (1,)), ((), ()))
FIRST = (((0,), (0,)), ((), ()))
MESH = pl.DeviceIdType.MESH
F32 = jnp.float32
BF16 = jnp.bfloat16


def group_index():
    return lax.axis_index("phase") * lax.axis_size("dp") + lax.axis_index("dp")


def peer_id(group):
    dp = lax.axis_size("dp")
    return {"phase": group // dp, "dp": lax.rem(group, dp)}


def greet_group(barrier, groups):
    me = group_index()

    def greet(k, carry):
        pl.semaphore_signal(
            barrier, inc=1, device_id=peer_id(lax.rem(me + k, groups)), device_id_type=MESH
        )
        return carry

    lax.fori_loop(1, groups, greet, 0)


def send_to_group(groups, source, target, send_sem, recv_sem):
    me = group_index()

    def copy_to(k):
        peer = lax.rem(me + k, groups)
        return pltpu.make_async_remote_copy(
            src_ref=source(peer),
            dst_ref=target.at[me],
            send_sem=send_sem.at[k],
            recv_sem=recv_sem.at[k],
            device_id=peer_id(peer),
            device_id_type=MESH,
        )

    def copy_from(k):
        peer = lax.rem(me + groups - k, groups)
        return pltpu.make_async_remote_copy(
            src_ref=source(peer),
            dst_ref=target.at[peer],
            send_sem=send_sem.at[k],
            recv_sem=recv_sem.at[k],
            device_id=peer_id(peer),
            device_id_type=MESH,
        )

    def start():
        lax.fori_loop(1, groups, lambda k, c: (copy_to(k).start(), c)[1], 0)

    def wait():
        def one(k, carry):
            copy_from(k).wait_recv()
            copy_to(k).wait_send()
            return carry

        lax.fori_loop(1, groups, one, 0)

    return start, wait


def project_kernel(
    groups, plan, queries, grads, encoded, key_weight, value_weight,
    keys, values, slots,
    outgoing, own, before, after, far, key_w, value_w, key_acc, value_acc,
    load_sem, ring_send, ring_recv, send_sem, recv_sem, local_sem,
):
    me = group_index()
    z = lax.axis_index("mp")
    ring = lax.axis_size("mp")
    up, down = lax.rem(z + 1, ring), lax.rem(z + ring - 1, ring)
    across = lax.rem(z + 2, ring)
    blocks = encoded.shape[0]
    half = blocks // 2

    barrier = pltpu.get_barrier_semaphore()
    pl.semaphore_signal(barrier, inc=1, device_id={"mp": up}, device_id_type=MESH)
    pl.semaphore_signal(barrier, inc=1, device_id={"mp": down}, device_id_type=MESH)
    greet_group(barrier, groups)

    own_load = pltpu.make_async_copy(encoded, own, load_sem.at[0])
    own_load.start()
    weight_loads = []
    for i, owner in enumerate((z, down, up, across)):
        pair = (
            pltpu.make_async_copy(key_weight.at[owner], key_w.at[i], load_sem.at[1 + 2 * i]),
            pltpu.make_async_copy(value_weight.at[owner], value_w.at[i], load_sem.at[2 + 2 * i]),
        )
        for load in pair:
            load.start()
        weight_loads.append(pair)

    def fill(o, carry):
        span = plan[groups + o]
        live = plan[2 * groups + o] > 0
        outgoing[o, 0] = jnp.where(live, queries[span], jnp.zeros_like(queries[span]))
        outgoing[o, 1] = jnp.where(live, grads[span], jnp.zeros_like(grads[span]))
        return carry

    lax.fori_loop(0, groups, fill, 0)

    def ring_copy(lane, source, target, block, to):
        return pltpu.make_async_remote_copy(
            src_ref=source.at[block],
            dst_ref=target.at[block],
            send_sem=ring_send.at[lane, block],
            recv_sem=ring_recv.at[lane, block],
            device_id={"mp": to},
            device_id_type=MESH,
        )

    def go_up(c):
        return ring_copy(0, encoded, before, c, up)

    def go_down(c):
        return ring_copy(1, encoded, after, c, down)

    def pass_up(c):
        return ring_copy(2, before, far, c, up)

    def pass_down(c):
        return ring_copy(2, after, far, c, down)

    pl.semaphore_wait(barrier, groups - 1 + 2)

    def send_own(c, carry):
        go_up(c).start()
        go_down(blocks - 1 - c).start()
        return carry

    lax.fori_loop(0, blocks, send_own, 0)
    start_slots, wait_slots = send_to_group(
        groups, lambda g: outgoing.at[g], slots, send_sem, recv_sem
    )
    start_slots()
    local = pltpu.make_async_copy(outgoing.at[me], slots.at[me], local_sem)
    local.start()

    def project(block, i):
        return (
            jnp.dot(block, key_w[i], preferred_element_type=F32),
            jnp.dot(block, value_w[i], preferred_element_type=F32),
        )

    def add(source, c, i):
        k, v = project(source[c], i)
        key_acc[c] += k
        value_acc[c] += v

    def finish(c):
        k, v = project(far[c], 3)
        keys[c] = (key_acc[c] + k).astype(BF16)
        values[c] = (value_acc[c] + v).astype(BF16)

    own_load.wait()
    for load in weight_loads[0]:
        load.wait()

    def first(c, carry):
        k, v = project(own[c], 0)
        key_acc[c] = k
        value_acc[c] = v
        return carry

    lax.fori_loop(0, blocks, first, 0)
    for pair in weight_loads[1:]:
        for load in pair:
            load.wait()

    def near(c, carry):
        d = blocks - 1 - c
        go_up(c).wait_recv()
        pass_up(c).start()
        go_down(d).wait_recv()
        pass_down(d).start()
        add(before, c, 1)
        add(after, d, 2)
        return carry

    lax.fori_loop(0, half, near, 0)

    def rest(c, carry):
        d = blocks - 1 - c
        go_up(c).wait_recv()
        add(before, c, 1)
        go_down(d).wait_recv()
        add(after, d, 2)
        return carry

    lax.fori_loop(half, blocks, rest, 0)

    def last(c, carry):
        d = blocks - 1 - c
        pass_up(c).wait_recv()
        finish(c)
        pass_down(d).wait_recv()
        finish(d)
        return carry

    lax.fori_loop(0, half, last, 0)

    def sent(c, carry):
        go_up(c).wait_send()
        go_down(c).wait_send()
        return carry

    lax.fori_loop(0, blocks, sent, 0)

    def passed(c, carry):
        pass_up(c).wait_send()
        pass_down(blocks - 1 - c).wait_send()
        return carry

    lax.fori_loop(0, half, passed, 0)
    wait_slots()
    local.wait()


def pair_operands(plan, pair, keys, values, slots, first, h):
    cols = pl.ds(h * HS, HS)
    top = lax.broadcasted_iota(jnp.int32, (2 * CLEN, HS), 0) < CLEN
    low, high = plan[2 * pair], plan[2 * pair + 1]

    def diagonal(which):
        block = slots[pl.ds(first, 2), which, :, cols].reshape(2 * CLEN, HS)
        zero = jnp.zeros_like(block)
        return jnp.concatenate([jnp.where(top, block, zero), jnp.where(top, zero, block)], 1)

    k = jnp.concatenate([keys[low, :, cols], keys[high, :, cols]], 1)
    v = jnp.concatenate([values[low, :, cols], values[high, :, cols]], 1)
    return k, v, diagonal(0), diagonal(1)


def attend_kernel(
    groups, plan, keys, values, slots, factors,
    stats, fetched, combined, back, landed,
    stat_send, stat_recv, back_send, back_recv, local_sem,
):
    me = group_index()
    heads = keys.shape[2] // HS
    spans = combined.shape[0]
    barrier = pltpu.get_barrier_semaphore()
    greet_group(barrier, groups)

    def one_pair(p, carry):
        for h in range(heads):
            k, v, q, g = pair_operands(plan, p, keys, values, slots, 2 * p, h)
            scores = lax.dot_general(k, q, LAST, preferred_element_type=F32) * SCALE
            grad_p = lax.dot_general(v, g, LAST, preferred_element_type=F32)
            peak = jnp.max(scores, 0, keepdims=True)
            weights = jnp.exp(scores - peak)
            stats[p, h : h + 1] = peak
            stats[p, heads + h : heads + h + 1] = jnp.sum(weights, 0, keepdims=True)
            stats[p, 2 * heads + h : 2 * heads + h + 1] = jnp.sum(
                weights * grad_p, 0, keepdims=True
            )
        stats[p, 3 * heads :] = jnp.zeros((stats.shape[1] - 3 * heads, 2 * CLEN), F32)
        return carry

    lax.fori_loop(0, groups // 2, one_pair, 0)
    pl.semaphore_wait(barrier, groups - 1)

    start, wait = send_to_group(
        groups, lambda g: stats.at[g // 2], fetched, stat_send, stat_recv
    )
    start()
    local = pltpu.make_async_copy(stats.at[me // 2], fetched.at[me], local_sem.at[0])
    local.start()
    local.wait()
    wait()

    def combine(t, carry):
        a = fetched[plan[3 * groups + 2 * t]]
        b = fetched[plan[3 * groups + 2 * t + 1]]
        overall = jnp.maximum(a[:heads], b[:heads])
        fa, fb = jnp.exp(a[:heads] - overall), jnp.exp(b[:heads] - overall)
        total = fa * a[heads : 2 * heads] + fb * b[heads : 2 * heads]
        grad = fa * a[2 * heads : 3 * heads] + fb * b[2 * heads : 3 * heads]
        combined[t, :heads] = overall + jnp.log(total)
        combined[t, heads:] = grad / total
        return carry

    lax.fori_loop(0, spans, combine, 0)

    def answer(o, carry):
        mine = combined[plan[groups + o]]
        back[o] = jnp.where(plan[2 * groups + o] > 0, mine, jnp.zeros_like(mine))
        return carry

    lax.fori_loop(0, groups, answer, 0)
    start, wait = send_to_group(groups, lambda g: back.at[g], landed, back_send, back_recv)
    start()
    local = pltpu.make_async_copy(back.at[me], landed.at[me], local_sem.at[1])
    local.start()
    local.wait()
    wait()
    left = lax.broadcasted_iota(jnp.int32, factors.shape[1:], 1) < CLEN

    def merge(p, carry):
        factors[p] = jnp.where(left, landed[2 * p], landed[2 * p + 1])
        return carry

    lax.fori_loop(0, groups // 2, merge, 0)


def grads_kernel(
    pairs, plan, factors, keys, values, slots, results, grad_keys, grad_values, key_acc, value_acc
):
    heads = keys.shape[2] // HS
    step = pl.program_id(0)

    @pl.when(step == 0)
    def _():
        key_acc[...] = jnp.zeros_like(key_acc)
        value_acc[...] = jnp.zeros_like(value_acc)

    top = lax.broadcasted_iota(jnp.int32, (2 * CLEN, HS), 0) < CLEN

    def one_pair(i, carry):
        p = step * pairs + i
        low, high = plan[2 * p], plan[2 * p + 1]
        for h in range(heads):
            cols = pl.ds(h * HS, HS)
            k, v, q, g = pair_operands(plan, p, keys, values, slots, 2 * i, h)
            scores = lax.dot_general(k, q, LAST, preferred_element_type=F32) * SCALE
            grad_p = lax.dot_general(v, g, LAST, preferred_element_type=F32)
            probs = jnp.exp(scores - factors[i, h : h + 1])
            grad_s = (probs * (grad_p - factors[i, heads + h : heads + h + 1])).astype(BF16)
            probs = probs.astype(BF16)
            grad_v = jnp.dot(probs, g, preferred_element_type=F32)
            grad_k = jnp.dot(grad_s, q, preferred_element_type=F32) * SCALE
            key_acc[low, :, cols] += grad_k[:, :HS]
            key_acc[high, :, cols] += grad_k[:, HS:]
            value_acc[low, :, cols] += grad_v[:, :HS]
            value_acc[high, :, cols] += grad_v[:, HS:]
            out = lax.dot_general(probs, v, FIRST, preferred_element_type=F32)
            grad_q = lax.dot_general(grad_s, k, FIRST, preferred_element_type=F32) * SCALE
            for j, both in enumerate((out, grad_q)):
                picked = jnp.where(top, both[:, :HS], both[:, HS:]).astype(BF16)
                results[pl.ds(2 * i, 2), j, :, cols] = picked.reshape(2, CLEN, HS)
        return carry

    lax.fori_loop(0, pairs, one_pair, 0)

    @pl.when(step == pl.num_programs(0) - 1)
    def _():
        grad_keys[...] = key_acc[...].astype(BF16)
        grad_values[...] = value_acc[...].astype(BF16)


def reduce_kernel(
    groups, plan, results, grad_keys, grad_values, key_weight, value_weight,
    attended, grad_q, grad_e,
    fetched, key_w, value_w, to_across, to_up, to_down, from_far, before, after, total,
    load_sem, ring_send, ring_recv, send_sem, recv_sem, local_sem,
):
    me = group_index()
    z = lax.axis_index("mp")
    ring = lax.axis_size("mp")
    up, down = lax.rem(z + 1, ring), lax.rem(z + ring - 1, ring)
    across = lax.rem(z + 2, ring)
    blocks = grad_keys.shape[0]
    half = blocks // 2
    spans = attended.shape[0]

    barrier = pltpu.get_barrier_semaphore()
    pl.semaphore_signal(barrier, inc=1, device_id={"mp": up}, device_id_type=MESH)
    pl.semaphore_signal(barrier, inc=1, device_id={"mp": down}, device_id_type=MESH)
    weight_loads = []
    for i, owner in enumerate((across, up, down, z)):
        pair = (
            pltpu.make_async_copy(key_weight.at[owner], key_w.at[i], load_sem.at[2 * i]),
            pltpu.make_async_copy(value_weight.at[owner], value_w.at[i], load_sem.at[2 * i + 1]),
        )
        for load in pair:
            load.start()
        weight_loads.append(pair)
    greet_group(barrier, groups)

    def part(c, i):
        return lax.dot_general(
            grad_keys[c], key_w[i], LAST, preferred_element_type=F32
        ) + lax.dot_general(grad_values[c], value_w[i], LAST, preferred_element_type=F32)

    def ring_copy(lane, source, target, block, to):
        return pltpu.make_async_remote_copy(
            src_ref=source.at[block],
            dst_ref=target.at[block],
            send_sem=ring_send.at[lane, block],
            recv_sem=ring_recv.at[lane, block],
            device_id={"mp": to},
            device_id_type=MESH,
        )

    def far_up(c):
        return ring_copy(2, to_across, from_far, c, up)

    def far_down(c):
        return ring_copy(2, to_across, from_far, c, down)

    def go_up(c):
        return ring_copy(0, to_up, before, c, up)

    def go_down(c):
        return ring_copy(1, to_down, after, c, down)

    pl.semaphore_wait(barrier, groups - 1 + 2)
    for load in weight_loads[0]:
        load.wait()

    def send_far(c, carry):
        d = blocks - 1 - c
        to_across[c] = part(c, 0).astype(BF16)
        far_up(c).start()
        to_across[d] = part(d, 0).astype(BF16)
        far_down(d).start()
        return carry

    lax.fori_loop(0, half, send_far, 0)
    start_results, wait_results = send_to_group(
        groups, lambda g: results.at[g], fetched, send_sem, recv_sem
    )
    start_results()
    local = pltpu.make_async_copy(results.at[me], fetched.at[me], local_sem)
    local.start()
    for pair in weight_loads[1:]:
        for load in pair:
            load.wait()

    def send_near(c, carry):
        d = blocks - 1 - c
        to_up[c] = part(c, 1).astype(BF16)
        go_up(c).start()
        to_down[d] = part(d, 2).astype(BF16)
        go_down(d).start()
        return carry

    lax.fori_loop(half, blocks, send_near, 0)

    def send_joined(c, carry):
        d = blocks - 1 - c
        mine = part(c, 1)
        far_up(c).wait_recv()
        to_up[c] = (mine + from_far[c].astype(F32)).astype(BF16)
        go_up(c).start()
        mine = part(d, 2)
        far_down(d).wait_recv()
        to_down[d] = (mine + from_far[d].astype(F32)).astype(BF16)
        go_down(d).start()
        return carry

    lax.fori_loop(0, half, send_joined, 0)

    def own(c, carry):
        total[c] = part(c, 3)
        return carry

    lax.fori_loop(0, blocks, own, 0)

    def add_first(c, carry):
        d = blocks - 1 - c
        go_up(c).wait_recv()
        total[c] += before[c].astype(F32)
        go_down(d).wait_recv()
        total[d] += after[d].astype(F32)
        return carry

    lax.fori_loop(half, blocks, add_first, 0)
    local.wait()
    wait_results()

    def finish_span(t, carry):
        a = plan[3 * groups + 2 * t]
        b = plan[3 * groups + 2 * t + 1]
        attended[t] = (fetched[a, 0].astype(F32) + fetched[b, 0].astype(F32)).astype(BF16)
        grad_q[t] = (fetched[a, 1].astype(F32) + fetched[b, 1].astype(F32)).astype(BF16)
        return carry

    lax.fori_loop(0, spans, finish_span, 0)

    def add_last(c, carry):
        d = blocks - 1 - c
        go_up(c).wait_recv()
        grad_e[c] = (total[c] + before[c].astype(F32)).astype(BF16)
        go_down(d).wait_recv()
        grad_e[d] = (total[d] + after[d].astype(F32)).astype(BF16)
        return carry

    lax.fori_loop(0, half, add_last, 0)

    def sent(c, carry):
        go_up(c).wait_send()
        go_down(c).wait_send()
        return carry

    lax.fori_loop(0, blocks, sent, 0)

    def sent_far(c, carry):
        far_up(c).wait_send()
        far_down(blocks - 1 - c).wait_send()
        return carry

    lax.fori_loop(0, half, sent_far, 0)


def params(collective_id=None, mib=56):
    return pltpu.CompilerParams(
        collective_id=collective_id,
        has_side_effects=collective_id is not None,
        vmem_limit_bytes=mib << 20,
    )


def body(queries, grad_out, encoded, key_weight, value_weight, send_rows, read_slots):
    groups = lax.axis_size(("phase", "dp"))
    ring = lax.axis_size("mp")
    blocks, _, features = encoded.shape
    width = key_weight.shape[1]
    heads = width // HS
    spans = read_slots.shape[0]
    hbm = pl.BlockSpec(memory_space=pl.ANY)
    vmem = pl.BlockSpec(memory_space=pltpu.VMEM)
    smem = pl.BlockSpec(memory_space=pltpu.SMEM)
    dma = pltpu.SemaphoreType.DMA

    reads = read_slots.reshape(2 * spans)
    matches = reads[None, :] == jnp.arange(groups, dtype=jnp.int32)[:, None]
    source = jnp.sum(
        jnp.where(matches, jnp.arange(2 * spans, dtype=jnp.int32)[None, :] // 2, 0), 1
    )
    live = jnp.any(matches, 1).astype(jnp.int32)
    plan = jnp.concatenate([send_rows.reshape(groups), source, live, reads])

    query_spans = queries.reshape(spans, CLEN, width)
    grad_spans = grad_out.reshape(spans, CLEN, width)
    key_parts = key_weight.reshape(ring, features, width)
    value_parts = value_weight.reshape(ring, features, width)

    keys, values, slots = pl.pallas_call(
        functools.partial(project_kernel, groups),
        out_shape=(
            jax.ShapeDtypeStruct((blocks, NLEN, width), BF16),
            jax.ShapeDtypeStruct((blocks, NLEN, width), BF16),
            jax.ShapeDtypeStruct((groups, 2, CLEN, width), BF16),
        ),
        in_specs=[smem, vmem, vmem, hbm, hbm, hbm],
        out_specs=(vmem, vmem, hbm),
        scratch_shapes=[
            pltpu.VMEM((groups, 2, CLEN, width), BF16),
            pltpu.VMEM(encoded.shape, BF16),
            pltpu.VMEM(encoded.shape, BF16),
            pltpu.VMEM(encoded.shape, BF16),
            pltpu.VMEM(encoded.shape, BF16),
            pltpu.VMEM(key_parts.shape, BF16),
            pltpu.VMEM(key_parts.shape, BF16),
            pltpu.VMEM((blocks, NLEN, width), F32),
            pltpu.VMEM((blocks, NLEN, width), F32),
            dma((9,)),
            dma((3, blocks)),
            dma((3, blocks)),
            dma((groups,)),
            dma((groups,)),
            dma,
        ],
        compiler_params=params(0),
        name="project",
    )(plan, query_spans, grad_spans, encoded, key_parts, value_parts)

    stat_rows = 16
    factors = pl.pallas_call(
        functools.partial(attend_kernel, groups),
        out_shape=jax.ShapeDtypeStruct((groups // 2, 2 * heads, 2 * CLEN), F32),
        in_specs=[smem, vmem, vmem, vmem],
        out_specs=vmem,
        scratch_shapes=[
            pltpu.VMEM((groups // 2, stat_rows, 2 * CLEN), F32),
            pltpu.VMEM((groups, stat_rows, 2 * CLEN), F32),
            pltpu.VMEM((spans, 2 * heads, 2 * CLEN), F32),
            pltpu.VMEM((groups, 2 * heads, 2 * CLEN), F32),
            pltpu.VMEM((groups, 2 * heads, 2 * CLEN), F32),
            dma((groups,)),
            dma((groups,)),
            dma((groups,)),
            dma((groups,)),
            dma((2,)),
        ],
        compiler_params=params(1),
        name="attend",
    )(plan, keys, values, slots)

    steps = 4
    pairs = groups // 2 // steps
    whole = pl.BlockSpec((blocks, NLEN, width), lambda i, plan: (0, 0, 0))
    per_step = pl.BlockSpec((2 * pairs, 2, CLEN, width), lambda i, plan: (i, 0, 0, 0))
    results, grad_keys, grad_values = pl.pallas_call(
        functools.partial(grads_kernel, pairs),
        out_shape=(
            jax.ShapeDtypeStruct((groups, 2, CLEN, width), BF16),
            jax.ShapeDtypeStruct((blocks, NLEN, width), BF16),
            jax.ShapeDtypeStruct((blocks, NLEN, width), BF16),
        ),
        grid_spec=pltpu.PrefetchScalarGridSpec(
            num_scalar_prefetch=1,
            grid=(steps,),
            in_specs=[
                pl.BlockSpec((pairs, 2 * heads, 2 * CLEN), lambda i, plan: (i, 0, 0)),
                whole,
                whole,
                per_step,
            ],
            out_specs=(per_step, whole, whole),
            scratch_shapes=[
                pltpu.VMEM((blocks, NLEN, width), F32),
                pltpu.VMEM((blocks, NLEN, width), F32),
            ],
        ),
        compiler_params=params(),
        name="grads",
    )(plan, factors, keys, values, slots)

    attended, grad_q, grad_e = pl.pallas_call(
        functools.partial(reduce_kernel, groups),
        out_shape=(
            jax.ShapeDtypeStruct((spans, CLEN, width), BF16),
            jax.ShapeDtypeStruct((spans, CLEN, width), BF16),
            jax.ShapeDtypeStruct(encoded.shape, BF16),
        ),
        in_specs=[smem, hbm, vmem, vmem, hbm, hbm],
        out_specs=(vmem, vmem, vmem),
        scratch_shapes=[
            pltpu.VMEM((groups, 2, CLEN, width), BF16),
            pltpu.VMEM(key_parts.shape, BF16),
            pltpu.VMEM(key_parts.shape, BF16),
            pltpu.VMEM(encoded.shape, BF16),
            pltpu.VMEM(encoded.shape, BF16),
            pltpu.VMEM(encoded.shape, BF16),
            pltpu.VMEM(encoded.shape, BF16),
            pltpu.VMEM(encoded.shape, BF16),
            pltpu.VMEM(encoded.shape, BF16),
            pltpu.VMEM(encoded.shape, F32),
            dma((8,)),
            dma((3, blocks)),
            dma((3, blocks)),
            dma((groups,)),
            dma((groups,)),
            dma,
        ],
        compiler_params=params(2),
        name="reduce",
    )(plan, results, grad_keys, grad_values, key_parts, value_parts)
    return (attended.reshape(queries.shape), grad_q.reshape(queries.shape), grad_e)


def solution(mesh):
    return jax.shard_map(
        body,
        mesh=mesh,
        in_specs=(
            P(("phase", "dp"), "mp"),
            P(("phase", "dp"), "mp"),
            P(("phase", "dp"), None, "mp"),
            P(None, "mp"),
            P(None, "mp"),
            P(("phase", "dp"), None, None),
            P(("phase", "dp"), None),
        ),
        out_specs=(
            P(("phase", "dp"), "mp"),
            P(("phase", "dp"), "mp"),
            P(("phase", "dp"), None, "mp"),
        ),
        check_vma=False,
    )
```

time: 598 us -> 218 us (0.36); the launches traced: 590 us -> 218 us
  waiting for transfers between devices: 344 us -> 0 us
  Pallas kernels: 0 us -> 208 us
  matrix products: 80.7 us -> 0 us
  blocking collectives: 56.6 us -> 0 us
  local copies, waits for them, and re-layouts: 58.8 us -> 7.65 us
  starting transfers between devices: 18 us -> 0 us
  other arithmetic: 16.7 us -> 1.44 us
  between operations: 14.8 us -> 0.66 us
    pallas_call x0 -> x4, Pallas kernels: none -> 208 us  [the longest x1 81.4 us: body(): pl.pallas_call(functools.partial(project_kernel, groups), out_shape=(jax....]
    reduce_scatter x1 -> x0, waiting for transfers between devices: 133 us -> none  [body(): lax.psum_scatter(lax.dot_general(key_row_list, grad_k_rows, contract, pre...]
    all_to_all x3 -> x0, waiting for transfers between devices: 125 us -> none  [the longest x1 48.6 us: body(): lax.all_to_all(grad_v_slots.reshape(groups, capacity, NLEN, heads_here *...]
    all_gather x1 -> x0, waiting for transfers between devices: 86 us -> none  [body(): pieces = lax.all_gather(rows_flat, 'mp', axis=1, tiled=True)]
    dot_general x12 -> x0, matrix products: 80.7 us -> none  [the longest x1 12.9 us: body(): lax.dot_general(key_row_list, grad_k_rows, contract, preferred_element_ty...]
    all_to_all x1 -> x0, blocking collectives: 56.6 us -> none  [body(): lax.all_to_all(outgoing[0], ('phase', 'dp'), split_axis=0, concat_axis=0,...]
    all_to_all x3 -> x0, starting transfers between devices: 17.9 us -> none  [the longest x1 7.36 us: body(): lax.all_to_all(outgoing[1], ('phase', 'dp'), split_axis=0, concat_axis=0,...]
    gather x10 -> x0, local copies, waits for them, and re-layouts: 16.8 us -> none  [the longest x4 4.31 us: to_slots(): gathered_rows = jnp.take(per_span, source_span, axis=0)]
  transfers between devices with their start and end apart: 5 -> 0, of which waited for: 5 -> 0; matrix products, arithmetic and copies ran while one was open for 9% -> 0% of each run, Pallas kernels for 0% -> 0%
where the time goes in v1:
time: 218 us
  Pallas kernels  208 us (95%)
  local copies, waits for them, and re-layouts  7.65 us (4%)
    pallas_call x1, Pallas kernels, body(): pl.pallas_call(functools.partial(project_kernel, groups), out_shape=(jax....  81.4 us
    pallas_call x1, Pallas kernels, body(): pl.pallas_call(functools.partial(reduce_kernel, groups), out_shape=(jax.S...  80.1 us
    pallas_call x1, Pallas kernels, body(): pl.pallas_call(functools.partial(grads_kernel, pairs), out_shape=(jax.Sha...  23.9 us
    pallas_call x1, Pallas kernels, body(): pl.pallas_call(functools.partial(attend_kernel, groups), out_shape=jax.Sh...  22.6 us
    unnamed x4, local copies, waits for them, and re-layouts  7.57 us

profile of v1, /device:TPU:16, one launch (start us, length us, event | category | flops | bytes accessed | tf_op | source)
XLA Modules:
  0.0 217.7 jit_solution(5074470083855608501)
XLA Ops:
  0.6 0.8 copy.12
  1.4 0.1 eq.15
  1.5 0.1 select_reduce_fusion
  1.6 0.1 fusion
  1.7 1.2 pad_add_fusion.plan
  2.9 81.4 %project.1 = (bf16[8,128,512]{2,1,0:T(8,128)(2,1)}, bf16[8,128,512]{2,1,0:T(8,128)(2,1)}, bf16[32,2,64,512]{3,2,1,0:T(8,128)(2,1)}) custom-call(s32[112]{0:T(128)} %pad_add_fusion.plan, bf16[8,64,512]{2,1,0:T(8,128)(2,1)} %bitcast.11, bf16[8,64,512]{2,1,0:T(8,128)(2,1)} %bitcast.12, bf16[8,128,1024]{2,1,0:T(8,128)(2,1)} %encoded.1, ...), custom_call_target="tpu_custom_call" | custom-call | tf_op jit(solution)/shard_map/project/pallas_call | solution.py:558
  84.4 22.6 %attend.1.factors = f32[16,8,128]{2,1,0:T(8,128)} custom-call(s32[112]{0:T(128)} %pad_add_fusion.plan, bf16[8,128,512]{2,1,0:T(8,128)(2,1)} %get-tuple-element.12.keys, bf16[8,128,512]{2,1,0:T(8,128)(2,1)} %get-tuple-element.13.values, bf16[32,2,64,512]{3,2,1,0:T(8,128)(2,1)} %get-tuple-element.14.slots), custom_call_target="tpu_custom_call" | custom-call | tf_op jit(solution)/shard_map/attend/pallas_call | solution.py:589
  106.9 23.9 %grads.1 = (bf16[32,2,64,512]{3,2,1,0:T(8,128)(2,1)}, bf16[8,128,512]{2,1,0:T(8,128)(2,1)}, bf16[8,128,512]{2,1,0:T(8,128)(2,1)}) custom-call(s32[112]{0:T(128)} %pad_add_fusion.plan, f32[16,8,128]{2,1,0:T(8,128)} %attend.1.factors, bf16[8,128,512]{2,1,0:T(8,128)(2,1)} %get-tuple-element.12.keys, bf16[8,128,512]{2,1,0:T(8,128)(2,1)} %get-tuple-element.13.values, ...), custom_call_target="tpu_custom_call" | custom-call | tf_op jit(solution)/shard_map/grads/pallas_call | solution.py:614
  130.8 80.1 %reduce.1 = (bf16[8,64,512]{2,1,0:T(8,128)(2,1)}, bf16[8,64,512]{2,1,0:T(8,128)(2,1)}, bf16[8,128,1024]{2,1,0:T(8,128)(2,1)}) custom-call(s32[112]{0:T(128)} %pad_add_fusion.plan, bf16[32,2,64,512]{3,2,1,0:T(8,128)(2,1)} %get-tuple-element.15.results, bf16[8,128,512]{2,1,0:T(8,128)(2,1)} %get-tuple-element.16.grad_keys, ...), custom_call_target="tpu_custom_call" | custom-call | tf_op jit(solution)/shard_map/reduce/pallas_call | solution.py:640
  210.9 1.9 copy.16
  212.8 1.9 copy.17
  214.7 3.1 %copy.18 = bf16[8,128,1024]{2,1,0:T(8,128)(2,1)} copy(bf16[8,128,1024]{2,1,0:T(8,128)(2,1)} %get-tuple-element.26) | data formatting | bytes 4194304
  (2 shorter events, 0.0 us)

commit v2 on v1

--- a/solution.py
+++ b/solution.py
@@ -78,11 +78,28 @@
     return start, wait
 
 
+def diagonal(slots, first, which, cols):
+    top = lax.broadcasted_iota(jnp.int32, (2 * CLEN, HS), 0) < CLEN
+    block = slots[pl.ds(first, 2), which, :, cols].reshape(2 * CLEN, HS)
+    zero = jnp.zeros_like(block)
+    return jnp.concatenate([jnp.where(top, block, zero), jnp.where(top, zero, block)], 1)
+
+
+def pair_operands(rows, pair, keys, values, slots, first, h):
+    cols = pl.ds(h * HS, HS)
+    low, high = rows[0, 2 * pair], rows[0, 2 * pair + 1]
+    k = jnp.concatenate([keys[low, :, cols], keys[high, :, cols]], 1)
+    v = jnp.concatenate([values[low, :, cols], values[high, :, cols]], 1)
+    return k, v, diagonal(slots, first, 0, cols), diagonal(slots, first, 1, cols)
+
+
 def project_kernel(
-    groups, plan, queries, grads, encoded, key_weight, value_weight,
-    keys, values, slots,
-    outgoing, own, before, after, far, key_w, value_w, key_acc, value_acc,
+    groups, rows, reads, queries, grads, encoded, key_weight, value_weight,
+    keys, values, slots_out, probs, grad_s,
+    source, live, outgoing, slots, own, before, after, far, key_w, value_w, key_acc, value_acc,
+    stats, fetched, combined, back, landed, weights, grad_p,
     load_sem, ring_send, ring_recv, send_sem, recv_sem, local_sem,
+    stat_send, stat_recv, back_send, back_recv,
 ):
     me = group_index()
     z = lax.axis_index("mp")
@@ -109,15 +126,6 @@
             load.start()
         weight_loads.append(pair)
 
-    def fill(o, carry):
-        span = plan[groups + o]
-        live = plan[2 * groups + o] > 0
-        outgoing[o, 0] = jnp.where(live, queries[span], jnp.zeros_like(queries[span]))
-        outgoing[o, 1] = jnp.where(live, grads[span], jnp.zeros_like(grads[span]))
-        return carry
-
-    lax.fori_loop(0, groups, fill, 0)
-
     def ring_copy(lane, source, target, block, to):
         return pltpu.make_async_remote_copy(
             src_ref=source.at[block],
@@ -148,11 +156,28 @@
         return carry
 
     lax.fori_loop(0, blocks, send_own, 0)
+    spans = queries.shape[0]
+
+    def fill(o, carry):
+        span = jnp.int32(0)
+        found = jnp.int32(0)
+        for t in range(spans):
+            for j in range(2):
+                hit = (reads[j, t] == o).astype(jnp.int32)
+                span = jnp.maximum(span, hit * t)
+                found = jnp.maximum(found, hit)
+        source[o] = span
+        live[o] = found
+        outgoing[o, 0] = jnp.where(found > 0, queries[span], jnp.zeros_like(queries[span]))
+        outgoing[o, 1] = jnp.where(found > 0, grads[span], jnp.zeros_like(grads[span]))
+        return carry
+
+    lax.fori_loop(0, groups, fill, 0)
     start_slots, wait_slots = send_to_group(
         groups, lambda g: outgoing.at[g], slots, send_sem, recv_sem
     )
     start_slots()
-    local = pltpu.make_async_copy(outgoing.at[me], slots.at[me], local_sem)
+    local = pltpu.make_async_copy(outgoing.at[me], slots.at[me], local_sem.at[0])
     local.start()
 
     def project(block, i):
@@ -208,6 +233,11 @@
 
     lax.fori_loop(half, blocks, rest, 0)
 
+    wait_slots()
+    local.wait()
+    slots_copy = pltpu.make_async_copy(slots, slots_out, local_sem.at[1])
+    slots_copy.start()
+
     def last(c, carry):
         d = blocks - 1 - c
         pass_up(c).wait_recv()
@@ -218,79 +248,37 @@
 
     lax.fori_loop(0, half, last, 0)
 
-    def sent(c, carry):
-        go_up(c).wait_send()
-        go_down(c).wait_send()
-        return carry
-
-    lax.fori_loop(0, blocks, sent, 0)
-
-    def passed(c, carry):
-        pass_up(c).wait_send()
-        pass_down(blocks - 1 - c).wait_send()
-        return carry
-
-    lax.fori_loop(0, half, passed, 0)
-    wait_slots()
-    local.wait()
-
-
-def pair_operands(plan, pair, keys, values, slots, first, h):
-    cols = pl.ds(h * HS, HS)
-    top = lax.broadcasted_iota(jnp.int32, (2 * CLEN, HS), 0) < CLEN
-    low, high = plan[2 * pair], plan[2 * pair + 1]
-
-    def diagonal(which):
-        block = slots[pl.ds(first, 2), which, :, cols].reshape(2 * CLEN, HS)
-        zero = jnp.zeros_like(block)
-        return jnp.concatenate([jnp.where(top, block, zero), jnp.where(top, zero, block)], 1)
-
-    k = jnp.concatenate([keys[low, :, cols], keys[high, :, cols]], 1)
-    v = jnp.concatenate([values[low, :, cols], values[high, :, cols]], 1)
-    return k, v, diagonal(0), diagonal(1)
-
-
-def attend_kernel(
-    groups, plan, keys, values, slots, factors,
-    stats, fetched, combined, back, landed,
-    stat_send, stat_recv, back_send, back_recv, local_sem,
-):
-    me = group_index()
     heads = keys.shape[2] // HS
-    spans = combined.shape[0]
-    barrier = pltpu.get_barrier_semaphore()
-    greet_group(barrier, groups)
-
-    def one_pair(p, carry):
+
+    def score(p, carry):
         for h in range(heads):
-            k, v, q, g = pair_operands(plan, p, keys, values, slots, 2 * p, h)
+            k, v, q, g = pair_operands(rows, p, keys, values, slots, 2 * p, h)
             scores = lax.dot_general(k, q, LAST, preferred_element_type=F32) * SCALE
-            grad_p = lax.dot_general(v, g, LAST, preferred_element_type=F32)
+            gp = lax.dot_general(v, g, LAST, preferred_element_type=F32)
             peak = jnp.max(scores, 0, keepdims=True)
-            weights = jnp.exp(scores - peak)
+            w = jnp.exp(scores - peak)
             stats[p, h : h + 1] = peak
-            stats[p, heads + h : heads + h + 1] = jnp.sum(weights, 0, keepdims=True)
-            stats[p, 2 * heads + h : 2 * heads + h + 1] = jnp.sum(
-                weights * grad_p, 0, keepdims=True
-            )
+            stats[p, heads + h : heads + h + 1] = jnp.sum(w, 0, keepdims=True)
+            stats[p, 2 * heads + h : 2 * heads + h + 1] = jnp.sum(w * gp, 0, keepdims=True)
+            weights[p, h] = w
+            grad_p[p, h] = gp
         stats[p, 3 * heads :] = jnp.zeros((stats.shape[1] - 3 * heads, 2 * CLEN), F32)
         return carry
 
-    lax.fori_loop(0, groups // 2, one_pair, 0)
-    pl.semaphore_wait(barrier, groups - 1)
+    lax.fori_loop(0, groups // 2, score, 0, unroll=4)
 
     start, wait = send_to_group(
         groups, lambda g: stats.at[g // 2], fetched, stat_send, stat_recv
     )
     start()
-    local = pltpu.make_async_copy(stats.at[me // 2], fetched.at[me], local_sem.at[0])
+    local = pltpu.make_async_copy(stats.at[me // 2], fetched.at[me], local_sem.at[2])
     local.start()
     local.wait()
     wait()
 
     def combine(t, carry):
-        a = fetched[plan[3 * groups + 2 * t]]
-        b = fetched[plan[3 * groups + 2 * t + 1]]
+        a = fetched[reads[0, t]]
+        b = fetched[reads[1, t]]
         overall = jnp.maximum(a[:heads], b[:heads])
         fa, fb = jnp.exp(a[:heads] - overall), jnp.exp(b[:heads] - overall)
         total = fa * a[heads : 2 * heads] + fb * b[heads : 2 * heads]
@@ -299,33 +287,51 @@
         combined[t, heads:] = grad / total
         return carry
 
-    lax.fori_loop(0, spans, combine, 0)
+    lax.fori_loop(0, spans, combine, 0, unroll=8)
 
     def answer(o, carry):
-        mine = combined[plan[groups + o]]
-        back[o] = jnp.where(plan[2 * groups + o] > 0, mine, jnp.zeros_like(mine))
-        return carry
-
-    lax.fori_loop(0, groups, answer, 0)
+        mine = combined[source[o]]
+        back[o] = jnp.where(live[o] > 0, mine, jnp.zeros_like(mine))
+        return carry
+
+    lax.fori_loop(0, groups, answer, 0, unroll=8)
     start, wait = send_to_group(groups, lambda g: back.at[g], landed, back_send, back_recv)
     start()
-    local = pltpu.make_async_copy(back.at[me], landed.at[me], local_sem.at[1])
+    local = pltpu.make_async_copy(back.at[me], landed.at[me], local_sem.at[3])
     local.start()
     local.wait()
     wait()
-    left = lax.broadcasted_iota(jnp.int32, factors.shape[1:], 1) < CLEN
-
-    def merge(p, carry):
-        factors[p] = jnp.where(left, landed[2 * p], landed[2 * p + 1])
-        return carry
-
-    lax.fori_loop(0, groups // 2, merge, 0)
-
-
-def grads_kernel(
-    pairs, plan, factors, keys, values, slots, results, grad_keys, grad_values, key_acc, value_acc
-):
-    heads = keys.shape[2] // HS
+    left = lax.broadcasted_iota(jnp.int32, landed.shape[1:], 1) < CLEN
+
+    def normalise(p, carry):
+        both = jnp.where(left, landed[2 * p], landed[2 * p + 1])
+        for h in range(heads):
+            factor = jnp.exp(stats[p, h : h + 1] - both[h : h + 1])
+            pr = weights[p, h] * factor
+            probs[p, h] = pr.astype(BF16)
+            grad_s[p, h] = (pr * (grad_p[p, h] - both[heads + h : heads + h + 1])).astype(BF16)
+        return carry
+
+    lax.fori_loop(0, groups // 2, normalise, 0, unroll=2)
+    slots_copy.wait()
+
+    def sent(c, carry):
+        go_up(c).wait_send()
+        go_down(c).wait_send()
+        return carry
+
+    lax.fori_loop(0, blocks, sent, 0)
+
+    def passed(c, carry):
+        pass_up(c).wait_send()
+        pass_down(blocks - 1 - c).wait_send()
+        return carry
+
+    lax.fori_loop(0, half, passed, 0)
+
+
+def grads_kernel(pairs, rows, probs, grad_s, slots, grad_keys, grad_values, key_acc, value_acc):
+    heads = probs.shape[1]
     step = pl.program_id(0)
 
     @pl.when(step == 0)
@@ -333,44 +339,32 @@
         key_acc[...] = jnp.zeros_like(key_acc)
         value_acc[...] = jnp.zeros_like(value_acc)
 
-    top = lax.broadcasted_iota(jnp.int32, (2 * CLEN, HS), 0) < CLEN
-
     def one_pair(i, carry):
         p = step * pairs + i
-        low, high = plan[2 * p], plan[2 * p + 1]
+        low, high = rows[2 * p], rows[2 * p + 1]
         for h in range(heads):
             cols = pl.ds(h * HS, HS)
-            k, v, q, g = pair_operands(plan, p, keys, values, slots, 2 * i, h)
-            scores = lax.dot_general(k, q, LAST, preferred_element_type=F32) * SCALE
-            grad_p = lax.dot_general(v, g, LAST, preferred_element_type=F32)
-            probs = jnp.exp(scores - factors[i, h : h + 1])
-            grad_s = (probs * (grad_p - factors[i, heads + h : heads + h + 1])).astype(BF16)
-            probs = probs.astype(BF16)
-            grad_v = jnp.dot(probs, g, preferred_element_type=F32)
-            grad_k = jnp.dot(grad_s, q, preferred_element_type=F32) * SCALE
+            grad_v = jnp.dot(probs[i, h], diagonal(slots, 2 * i, 1, cols), preferred_element_type=F32)
+            grad_k = jnp.dot(grad_s[i, h], diagonal(slots, 2 * i, 0, cols), preferred_element_type=F32)
             key_acc[low, :, cols] += grad_k[:, :HS]
             key_acc[high, :, cols] += grad_k[:, HS:]
             value_acc[low, :, cols] += grad_v[:, :HS]
             value_acc[high, :, cols] += grad_v[:, HS:]
-            out = lax.dot_general(probs, v, FIRST, preferred_element_type=F32)
-            grad_q = lax.dot_general(grad_s, k, FIRST, preferred_element_type=F32) * SCALE
-            for j, both in enumerate((out, grad_q)):
-                picked = jnp.where(top, both[:, :HS], both[:, HS:]).astype(BF16)
-                results[pl.ds(2 * i, 2), j, :, cols] = picked.reshape(2, CLEN, HS)
-        return carry
-
-    lax.fori_loop(0, pairs, one_pair, 0)
+        return carry
+
+    lax.fori_loop(0, pairs, one_pair, 0, unroll=pairs)
 
     @pl.when(step == pl.num_programs(0) - 1)
     def _():
-        grad_keys[...] = key_acc[...].astype(BF16)
+        grad_keys[...] = (key_acc[...] * SCALE).astype(BF16)
         grad_values[...] = value_acc[...].astype(BF16)
 
 
 def reduce_kernel(
-    groups, plan, results, grad_keys, grad_values, key_weight, value_weight,
+    groups, rows, reads, keys, values, probs, grad_s, grad_keys, grad_values,
+    key_weight, value_weight,
     attended, grad_q, grad_e,
-    fetched, key_w, value_w, to_across, to_up, to_down, from_far, before, after, total,
+    results, fetched, key_w, value_w, to_across, to_up, to_down, from_far, before, after, total,
     load_sem, ring_send, ring_recv, send_sem, recv_sem, local_sem,
 ):
     me = group_index()
@@ -436,6 +430,22 @@
         return carry
 
     lax.fori_loop(0, half, send_far, 0)
+    top = lax.broadcasted_iota(jnp.int32, (2 * CLEN, HS), 0) < CLEN
+
+    def answers(p, carry):
+        low, high = rows[0, 2 * p], rows[0, 2 * p + 1]
+        for h in range(keys.shape[2] // HS):
+            cols = pl.ds(h * HS, HS)
+            k = jnp.concatenate([keys[low, :, cols], keys[high, :, cols]], 1)
+            v = jnp.concatenate([values[low, :, cols], values[high, :, cols]], 1)
+            out = lax.dot_general(probs[p, h], v, FIRST, preferred_element_type=F32)
+            gq = lax.dot_general(grad_s[p, h], k, FIRST, preferred_element_type=F32) * SCALE
+            for j, both in enumerate((out, gq)):
+                picked = jnp.where(top, both[:, :HS], both[:, HS:]).astype(BF16)
+                results[pl.ds(2 * p, 2), j, :, cols] = picked.reshape(2, CLEN, HS)
+        return carry
+
+    lax.fori_loop(0, groups // 2, answers, 0, unroll=2)
     start_results, wait_results = send_to_group(
         groups, lambda g: results.at[g], fetched, send_sem, recv_sem
     )
@@ -489,8 +499,7 @@
     wait_results()
 
     def finish_span(t, carry):
-        a = plan[3 * groups + 2 * t]
-        b = plan[3 * groups + 2 * t + 1]
+        a, b = reads[0, t], reads[1, t]
         attended[t] = (fetched[a, 0].astype(F32) + fetched[b, 0].astype(F32)).astype(BF16)
         grad_q[t] = (fetched[a, 1].astype(F32) + fetched[b, 1].astype(F32)).astype(BF16)
         return carry
@@ -520,6 +529,12 @@
         return carry
 
     lax.fori_loop(0, half, sent_far, 0)
+
+
+def finish_kernel(*refs):
+    count = len(refs) // 2
+    for source, target in zip(refs[:count], refs[count:]):
+        target[...] = source[...]
 
 
 def params(collective_id=None, mib=56):
@@ -541,31 +556,29 @@
     vmem = pl.BlockSpec(memory_space=pltpu.VMEM)
     smem = pl.BlockSpec(memory_space=pltpu.SMEM)
     dma = pltpu.SemaphoreType.DMA
-
-    reads = read_slots.reshape(2 * spans)
-    matches = reads[None, :] == jnp.arange(groups, dtype=jnp.int32)[:, None]
-    source = jnp.sum(
-        jnp.where(matches, jnp.arange(2 * spans, dtype=jnp.int32)[None, :] // 2, 0), 1
-    )
-    live = jnp.any(matches, 1).astype(jnp.int32)
-    plan = jnp.concatenate([send_rows.reshape(groups), source, live, reads])
-
+    half_pairs = groups // 2
+
+    rows = send_rows.reshape(1, groups)
+    reads = read_slots.T
     query_spans = queries.reshape(spans, CLEN, width)
     grad_spans = grad_out.reshape(spans, CLEN, width)
     key_parts = key_weight.reshape(ring, features, width)
     value_parts = value_weight.reshape(ring, features, width)
-
-    keys, values, slots = pl.pallas_call(
+    block_shape = jax.ShapeDtypeStruct((blocks, NLEN, width), BF16)
+    slot_shape = jax.ShapeDtypeStruct((groups, 2, CLEN, width), BF16)
+    prob_shape = jax.ShapeDtypeStruct((half_pairs, heads, NLEN, 2 * CLEN), BF16)
+
+    stat_rows = 16
+    keys, values, slots, probs, grad_s = pl.pallas_call(
         functools.partial(project_kernel, groups),
-        out_shape=(
-            jax.ShapeDtypeStruct((blocks, NLEN, width), BF16),
-            jax.ShapeDtypeStruct((blocks, NLEN, width), BF16),
-            jax.ShapeDtypeStruct((groups, 2, CLEN, width), BF16),
-        ),
-        in_specs=[smem, vmem, vmem, hbm, hbm, hbm],
-        out_specs=(vmem, vmem, hbm),
+        out_shape=(block_shape, block_shape, slot_shape, prob_shape, prob_shape),
+        in_specs=[smem, smem, vmem, vmem, hbm, hbm, hbm],
+        out_specs=(vmem, vmem, hbm, vmem, vmem),
         scratch_shapes=[
-            pltpu.VMEM((groups, 2, CLEN, width), BF16),
+            pltpu.SMEM((groups,), jnp.int32),
+            pltpu.SMEM((groups,), jnp.int32),
+            pltpu.VMEM(slot_shape.shape, BF16),
+            pltpu.VMEM(slot_shape.shape, BF16),
             pltpu.VMEM(encoded.shape, BF16),
             pltpu.VMEM(encoded.shape, BF16),
             pltpu.VMEM(encoded.shape, BF16),
@@ -574,80 +587,62 @@
             pltpu.VMEM(key_parts.shape, BF16),
             pltpu.VMEM((blocks, NLEN, width), F32),
             pltpu.VMEM((blocks, NLEN, width), F32),
+            pltpu.VMEM((half_pairs, stat_rows, 2 * CLEN), F32),
+            pltpu.VMEM((groups, stat_rows, 2 * CLEN), F32),
+            pltpu.VMEM((spans, 2 * heads, 2 * CLEN), F32),
+            pltpu.VMEM((groups, 2 * heads, 2 * CLEN), F32),
+            pltpu.VMEM((groups, 2 * heads, 2 * CLEN), F32),
+            pltpu.VMEM(prob_shape.shape, F32),
+            pltpu.VMEM(prob_shape.shape, F32),
             dma((9,)),
             dma((3, blocks)),
             dma((3, blocks)),
             dma((groups,)),
             dma((groups,)),
-            dma,
-        ],
-        compiler_params=params(0),
-        name="project",
-    )(plan, query_spans, grad_spans, encoded, key_parts, value_parts)
-
-    stat_rows = 16
-    factors = pl.pallas_call(
-        functools.partial(attend_kernel, groups),
-        out_shape=jax.ShapeDtypeStruct((groups // 2, 2 * heads, 2 * CLEN), F32),
-        in_specs=[smem, vmem, vmem, vmem],
-        out_specs=vmem,
-        scratch_shapes=[
-            pltpu.VMEM((groups // 2, stat_rows, 2 * CLEN), F32),
-            pltpu.VMEM((groups, stat_rows, 2 * CLEN), F32),
-            pltpu.VMEM((spans, 2 * heads, 2 * CLEN), F32),
-            pltpu.VMEM((groups, 2 * heads, 2 * CLEN), F32),
-            pltpu.VMEM((groups, 2 * heads, 2 * CLEN), F32),
+            dma((4,)),
             dma((groups,)),
             dma((groups,)),
             dma((groups,)),
             dma((groups,)),
-            dma((2,)),
         ],
-        compiler_params=params(1),
-        name="attend",
-    )(plan, keys, values, slots)
+        compiler_params=params(0),
+        name="project",
+    )(rows, reads, query_spans, grad_spans, encoded, key_parts, value_parts)
 
     steps = 4
-    pairs = groups // 2 // steps
-    whole = pl.BlockSpec((blocks, NLEN, width), lambda i, plan: (0, 0, 0))
-    per_step = pl.BlockSpec((2 * pairs, 2, CLEN, width), lambda i, plan: (i, 0, 0, 0))
-    results, grad_keys, grad_values = pl.pallas_call(
+    pairs = half_pairs // steps
+    whole = pl.BlockSpec(block_shape.shape, lambda i, rows: (0, 0, 0))
+    per_pair = pl.BlockSpec((pairs,) + prob_shape.shape[1:], lambda i, rows: (i, 0, 0, 0))
+    per_slot = pl.BlockSpec((2 * pairs,) + slot_shape.shape[1:], lambda i, rows: (i, 0, 0, 0))
+    grad_keys, grad_values = pl.pallas_call(
         functools.partial(grads_kernel, pairs),
-        out_shape=(
-            jax.ShapeDtypeStruct((groups, 2, CLEN, width), BF16),
-            jax.ShapeDtypeStruct((blocks, NLEN, width), BF16),
-            jax.ShapeDtypeStruct((blocks, NLEN, width), BF16),
-        ),
+        out_shape=(block_shape, block_shape),
         grid_spec=pltpu.PrefetchScalarGridSpec(
             num_scalar_prefetch=1,
             grid=(steps,),
-            in_specs=[
-                pl.BlockSpec((pairs, 2 * heads, 2 * CLEN), lambda i, plan: (i, 0, 0)),
-                whole,
-                whole,
-                per_step,
-            ],
-            out_specs=(per_step, whole, whole),
+            in_specs=[per_pair, per_pair, per_slot],
+            out_specs=(whole, whole),
             scratch_shapes=[
-                pltpu.VMEM((blocks, NLEN, width), F32),
-                pltpu.VMEM((blocks, NLEN, width), F32),
+                pltpu.VMEM(block_shape.shape, F32),
+                pltpu.VMEM(block_shape.shape, F32),
             ],
         ),
         compiler_params=params(),
         name="grads",
-    )(plan, factors, keys, values, slots)
-
-    attended, grad_q, grad_e = pl.pallas_call(
+    )(send_rows.reshape(groups), probs, grad_s, slots)
+
+    results = pl.pallas_call(
         functools.partial(reduce_kernel, groups),
         out_shape=(
             jax.ShapeDtypeStruct((spans, CLEN, width), BF16),
             jax.ShapeDtypeStruct((spans, CLEN, width), BF16),
             jax.ShapeDtypeStruct(encoded.shape, BF16),
         ),
-        in_specs=[smem, hbm, vmem, vmem, hbm, hbm],
+        in_specs=[smem, smem, vmem, vmem, vmem, vmem, vmem, vmem, hbm, hbm],
         out_specs=(vmem, vmem, vmem),
         scratch_shapes=[
-            pltpu.VMEM((groups, 2, CLEN, width), BF16),
+            pltpu.VMEM(slot_shape.shape, BF16),
+            pltpu.VMEM(slot_shape.shape, BF16),
             pltpu.VMEM(key_parts.shape, BF16),
             pltpu.VMEM(key_parts.shape, BF16),
             pltpu.VMEM(encoded.shape, BF16),
@@ -666,7 +661,20 @@
         ],
         compiler_params=params(2),
         name="reduce",
-    )(plan, results, grad_keys, grad_values, key_parts, value_parts)
+    )(rows, reads, keys, values, probs, grad_s, grad_keys, grad_values, key_parts, value_parts)
+    parts = 4
+    slices = [
+        pl.BlockSpec((r.shape[0] // parts,) + r.shape[1:], lambda i: (i, 0, 0)) for r in results
+    ]
+    attended, grad_q, grad_e = pl.pallas_call(
+        finish_kernel,
+        out_shape=tuple(jax.ShapeDtypeStruct(r.shape, r.dtype) for r in results),
+        grid=(parts,),
+        in_specs=slices,
+        out_specs=tuple(slices),
+        compiler_params=params(),
+        name="finish",
+    )(*results)
     return (attended.reshape(queries.shape), grad_q.reshape(queries.shape), grad_e)
 
 

time: 218 us -> 197 us (0.904)
  Pallas kernels: 208 us -> 196 us
  local copies, waits for them, and re-layouts: 7.65 us -> 0 us
    pallas_call x3, Pallas kernels: 128 us -> 112 us  [the longest x1 98.8 us: body(): pl.pallas_call(functools.partial(project_kernel, groups), out_shape=(bloc...]
    unnamed x4 -> x0, local copies, waits for them, and re-layouts: 7.57 us -> none
    pallas_call x1, Pallas kernels: 80.1 us -> 84.8 us  [body(): pl.pallas_call(functools.partial(reduce_kernel, groups), out_shape=(jax.S...]
where the time goes in v2:
time: 197 us
  Pallas kernels  196 us (99%)
    pallas_call x1, Pallas kernels, body(): pl.pallas_call(functools.partial(project_kernel, groups), out_shape=(bloc...  98.8 us
    pallas_call x1, Pallas kernels, body(): pl.pallas_call(functools.partial(reduce_kernel, groups), out_shape=(jax.S...  84.8 us
    pallas_call x1, Pallas kernels, body(): pl.pallas_call(functools.partial(grads_kernel, pairs), out_shape=(block_s...  8.62 us
    pallas_call x1, Pallas kernels, body(): pl.pallas_call(finish_kernel, out_shape=tuple((jax.ShapeDtypeStruct(r.sha...  4.23 us

profile of v2, /device:TPU:16, one launch (start us, length us, event | category | flops | bytes accessed | tf_op | source)
XLA Modules:
  0.0 197.1 jit_solution(4049183837390524551)
XLA Ops:
  0.6 98.8 %project.1 = (bf16[8,128,512]{2,1,0:T(8,128)(2,1)}, bf16[8,128,512]{2,1,0:T(8,128)(2,1)}, bf16[32,2,64,512]{3,2,1,0:T(8,128)(2,1)}, bf16[16,4,128,128]{3,2,1,0:T(8,128)(2,1)}, bf16[16,4,128,128]{3,2,1,0:T(8,128)(2,1)}) custom-call(s32[1,32]{1,0:T(1,128)} %bitcast.15, s32[2,8]{1,0:T(2,128)} %bitcast.18, bf16[8,64,512]{2,1,0:T(8,128)(2,1)} %bitcast.13, ...), custom_call_target="tpu_custom_call" | custom-call | tf_op jit(solution)/shard_map/project/pallas_call | solution.py:572
  99.4 8.6 %grads.1 = (bf16[8,128,512]{2,1,0:T(8,128)(2,1)}, bf16[8,128,512]{2,1,0:T(8,128)(2,1)}) custom-call(s32[32]{0:T(128)} %bitcast.16, bf16[16,4,128,128]{3,2,1,0:T(8,128)(2,1)} %get-tuple-element.18.probs, bf16[16,4,128,128]{3,2,1,0:T(8,128)(2,1)} %get-tuple-element.19.grad_s, bf16[32,2,64,512]{3,2,1,0:T(8,128)(2,1)} %get-tuple-element.20.slots), custom_call_target="tpu_custom_call" | custom-call | tf_op jit(solution)/shard_map/grads/pallas_call | solution.py:617
  108.0 84.8 %reduce.1 = (bf16[8,64,512]{2,1,0:T(8,128)(2,1)}, bf16[8,64,512]{2,1,0:T(8,128)(2,1)}, bf16[8,128,1024]{2,1,0:T(8,128)(2,1)}) custom-call(s32[1,32]{1,0:T(1,128)} %bitcast.17, s32[2,8]{1,0:T(2,128)} %bitcast.19, bf16[8,128,512]{2,1,0:T(8,128)(2,1)} %get-tuple-element.16.keys, bf16[8,128,512]{2,1,0:T(8,128)(2,1)} %get-tuple-element.17.values, ...), custom_call_target="tpu_custom_call" | custom-call | tf_op jit(solution)/shard_map/reduce/pallas_call | solution.py:634
  192.8 4.2 %finish.1 = (bf16[8,64,512]{2,1,0:T(8,128)(2,1)}, bf16[8,64,512]{2,1,0:T(8,128)(2,1)}, bf16[8,128,1024]{2,1,0:T(8,128)(2,1)}) custom-call(bf16[8,64,512]{2,1,0:T(8,128)(2,1)} %get-tuple-element.23.refs_0_, bf16[8,64,512]{2,1,0:T(8,128)(2,1)} %get-tuple-element.24.refs_1_, bf16[8,128,1024]{2,1,0:T(8,128)(2,1)} %get-tuple-element.25.refs_2_), custom_call_target="tpu_custom_call" | custom-call | tf_op jit(solution)/shard_map/finish/pallas_call | solution.py:669

commit v3 on v2

--- a/solution.py
+++ b/solution.py
@@ -93,13 +93,17 @@
     return k, v, diagonal(slots, first, 0, cols), diagonal(slots, first, 1, cols)
 
 
-def project_kernel(
+def retro_kernel(
     groups, rows, reads, queries, grads, encoded, key_weight, value_weight,
-    keys, values, slots_out, probs, grad_s,
-    source, live, outgoing, slots, own, before, after, far, key_w, value_w, key_acc, value_acc,
-    stats, fetched, combined, back, landed, weights, grad_p,
+    attended_out, grad_q_out, grad_e_out,
+    source, live, rank, order, keep, final, filled,
+    query_in, grad_in, outgoing, slots, own, before, after, far, key_w, value_w,
+    key_acc, value_acc, keys, values, probs, grad_s, weights, grad_p,
+    stats, fetched, combined, back, landed, key_run, value_run, value_sums,
+    answers_in, from_far, from_below, from_above,
     load_sem, ring_send, ring_recv, send_sem, recv_sem, local_sem,
     stat_send, stat_recv, back_send, back_recv,
+    sum_send, sum_recv, answer_send, answer_recv, out_sem,
 ):
     me = group_index()
     z = lax.axis_index("mp")
@@ -114,6 +118,12 @@
     pl.semaphore_signal(barrier, inc=1, device_id={"mp": down}, device_id_type=MESH)
     greet_group(barrier, groups)
 
+    inputs = (
+        pltpu.make_async_copy(queries, query_in, load_sem.at[9]),
+        pltpu.make_async_copy(grads, grad_in, load_sem.at[10]),
+    )
+    for load in inputs:
+        load.start()
     own_load = pltpu.make_async_copy(encoded, own, load_sem.at[0])
     own_load.start()
     weight_loads = []
@@ -168,10 +178,13 @@
                 found = jnp.maximum(found, hit)
         source[o] = span
         live[o] = found
-        outgoing[o, 0] = jnp.where(found > 0, queries[span], jnp.zeros_like(queries[span]))
-        outgoing[o, 1] = jnp.where(found > 0, grads[span], jnp.zeros_like(grads[span]))
-        return carry
-
+        for j, array in enumerate((query_in, grad_in)):
+            block = array[span]
+            outgoing[o, j] = jnp.where(found > 0, block, jnp.zeros_like(block))
+        return carry
+
+    for load in inputs:
+        load.wait()
     lax.fori_loop(0, groups, fill, 0)
     start_slots, wait_slots = send_to_group(
         groups, lambda g: outgoing.at[g], slots, send_sem, recv_sem
@@ -179,6 +192,43 @@
     start_slots()
     local = pltpu.make_async_copy(outgoing.at[me], slots.at[me], local_sem.at[0])
     local.start()
+
+    def place(o, carry):
+        mine = rows[0, o]
+        count = jnp.int32(0)
+        for other in range(groups):
+            theirs = rows[0, other]
+            count += (theirs < mine).astype(jnp.int32)
+            count += ((theirs == mine) & (other < o)).astype(jnp.int32)
+        rank[o] = count
+        return carry
+
+    def invert(i, carry):
+        slot = jnp.int32(0)
+        for o in range(groups):
+            slot = jnp.maximum(slot, (rank[o] == i).astype(jnp.int32) * o)
+        order[i] = slot
+        return carry
+
+    def follow(i, carry):
+        same = rows[0, order[i]] == rows[0, order[jnp.maximum(i - 1, 0)]]
+        keep[i] = (same & (i > 0)).astype(jnp.int32)
+        return carry
+
+    def close(n, carry):
+        upto = jnp.int32(0)
+        here = jnp.int32(0)
+        for o in range(groups):
+            upto += (rows[0, o] <= n).astype(jnp.int32)
+            here += (rows[0, o] == n).astype(jnp.int32)
+        final[n] = jnp.maximum(upto - 1, 0)
+        filled[n] = jnp.minimum(here, 1)
+        return carry
+
+    lax.fori_loop(0, groups, place, 0)
+    lax.fori_loop(0, groups, invert, 0)
+    lax.fori_loop(0, groups, follow, 0)
+    lax.fori_loop(0, blocks, close, 0)
 
     def project(block, i):
         return (
@@ -235,8 +285,6 @@
 
     wait_slots()
     local.wait()
-    slots_copy = pltpu.make_async_copy(slots, slots_out, local_sem.at[1])
-    slots_copy.start()
 
     def last(c, carry):
         d = blocks - 1 - c
@@ -313,7 +361,46 @@
         return carry
 
     lax.fori_loop(0, groups // 2, normalise, 0, unroll=2)
-    slots_copy.wait()
+
+    half_lane = lax.broadcasted_iota(jnp.int32, (NLEN, 2 * CLEN), 1) // CLEN
+    key_run[...] = jnp.zeros_like(key_run)
+    value_run[...] = jnp.zeros_like(value_run)
+
+    def accumulate(i, carry):
+        slot = order[i]
+        pair = slot // 2
+        mine = half_lane == lax.rem(slot, 2)
+        more = keep[i].astype(F32)
+        for h in range(heads):
+            cols = pl.ds(h * HS, HS)
+            zero = jnp.zeros((NLEN, 2 * CLEN), BF16)
+            p = jnp.where(mine, probs[pair, h], zero)
+            s = jnp.where(mine, grad_s[pair, h], zero)
+            q, g = slots[slot, 0, :, cols], slots[slot, 1, :, cols]
+            k = key_run[:, cols] * more + jnp.dot(
+                s, jnp.concatenate([q, q], 0), preferred_element_type=F32
+            )
+            v = value_run[:, cols] * more + jnp.dot(
+                p, jnp.concatenate([g, g], 0), preferred_element_type=F32
+            )
+            key_run[:, cols] = k
+            value_run[:, cols] = v
+            outgoing[i, :, :, cols] = (k * SCALE).astype(BF16).reshape(2, CLEN, HS)
+            value_sums[i, :, :, cols] = v.astype(BF16).reshape(2, CLEN, HS)
+        return carry
+
+    lax.fori_loop(0, groups, accumulate, 0, unroll=4)
+    width = keys.shape[2]
+
+    def gather(n, carry):
+        for j, sums in enumerate((outgoing, value_sums)):
+            block = sums[final[n]].reshape(NLEN, width)
+            far[n, :, j * width : (j + 1) * width] = jnp.where(
+                filled[n] > 0, block, jnp.zeros_like(block)
+            )
+        return carry
+
+    lax.fori_loop(0, blocks, gather, 0)
 
     def sent(c, carry):
         go_up(c).wait_send()
@@ -329,112 +416,50 @@
 
     lax.fori_loop(0, half, passed, 0)
 
-
-def grads_kernel(pairs, rows, probs, grad_s, slots, grad_keys, grad_values, key_acc, value_acc):
-    heads = probs.shape[1]
-    step = pl.program_id(0)
-
-    @pl.when(step == 0)
-    def _():
-        key_acc[...] = jnp.zeros_like(key_acc)
-        value_acc[...] = jnp.zeros_like(value_acc)
-
-    def one_pair(i, carry):
-        p = step * pairs + i
-        low, high = rows[2 * p], rows[2 * p + 1]
-        for h in range(heads):
-            cols = pl.ds(h * HS, HS)
-            grad_v = jnp.dot(probs[i, h], diagonal(slots, 2 * i, 1, cols), preferred_element_type=F32)
-            grad_k = jnp.dot(grad_s[i, h], diagonal(slots, 2 * i, 0, cols), preferred_element_type=F32)
-            key_acc[low, :, cols] += grad_k[:, :HS]
-            key_acc[high, :, cols] += grad_k[:, HS:]
-            value_acc[low, :, cols] += grad_v[:, :HS]
-            value_acc[high, :, cols] += grad_v[:, HS:]
-        return carry
-
-    lax.fori_loop(0, pairs, one_pair, 0, unroll=pairs)
-
-    @pl.when(step == pl.num_programs(0) - 1)
-    def _():
-        grad_keys[...] = (key_acc[...] * SCALE).astype(BF16)
-        grad_values[...] = value_acc[...].astype(BF16)
-
-
-def reduce_kernel(
-    groups, rows, reads, keys, values, probs, grad_s, grad_keys, grad_values,
-    key_weight, value_weight,
-    attended, grad_q, grad_e,
-    results, fetched, key_w, value_w, to_across, to_up, to_down, from_far, before, after, total,
-    load_sem, ring_send, ring_recv, send_sem, recv_sem, local_sem,
-):
-    me = group_index()
-    z = lax.axis_index("mp")
-    ring = lax.axis_size("mp")
-    up, down = lax.rem(z + 1, ring), lax.rem(z + ring - 1, ring)
-    across = lax.rem(z + 2, ring)
-    blocks = grad_keys.shape[0]
-    half = blocks // 2
-    spans = attended.shape[0]
-
-    barrier = pltpu.get_barrier_semaphore()
-    pl.semaphore_signal(barrier, inc=1, device_id={"mp": up}, device_id_type=MESH)
-    pl.semaphore_signal(barrier, inc=1, device_id={"mp": down}, device_id_type=MESH)
-    weight_loads = []
-    for i, owner in enumerate((across, up, down, z)):
-        pair = (
-            pltpu.make_async_copy(key_weight.at[owner], key_w.at[i], load_sem.at[2 * i]),
-            pltpu.make_async_copy(value_weight.at[owner], value_w.at[i], load_sem.at[2 * i + 1]),
-        )
-        for load in pair:
-            load.start()
-        weight_loads.append(pair)
-    greet_group(barrier, groups)
-
     def part(c, i):
         return lax.dot_general(
-            grad_keys[c], key_w[i], LAST, preferred_element_type=F32
-        ) + lax.dot_general(grad_values[c], value_w[i], LAST, preferred_element_type=F32)
-
-    def ring_copy(lane, source, target, block, to):
+            far[c, :, :width], key_w[i], LAST, preferred_element_type=F32
+        ) + lax.dot_general(far[c, :, width:], value_w[i], LAST, preferred_element_type=F32)
+
+    def sum_copy(lane, source, target, block, to):
         return pltpu.make_async_remote_copy(
             src_ref=source.at[block],
             dst_ref=target.at[block],
-            send_sem=ring_send.at[lane, block],
-            recv_sem=ring_recv.at[lane, block],
+            send_sem=sum_send.at[lane, block],
+            recv_sem=sum_recv.at[lane, block],
             device_id={"mp": to},
             device_id_type=MESH,
         )
 
+    to_across, to_up, to_down = own, before, after
+
     def far_up(c):
-        return ring_copy(2, to_across, from_far, c, up)
+        return sum_copy(2, to_across, from_far, c, up)
 
     def far_down(c):
-        return ring_copy(2, to_across, from_far, c, down)
-
-    def go_up(c):
-        return ring_copy(0, to_up, before, c, up)
-
-    def go_down(c):
-        return ring_copy(1, to_down, after, c, down)
-
-    pl.semaphore_wait(barrier, groups - 1 + 2)
-    for load in weight_loads[0]:
-        load.wait()
+        return sum_copy(2, to_across, from_far, c, down)
+
+    def sum_up(c):
+        return sum_copy(0, to_up, from_below, c, up)
+
+    def sum_down(c):
+        return sum_copy(1, to_down, from_above, c, down)
 
     def send_far(c, carry):
         d = blocks - 1 - c
-        to_across[c] = part(c, 0).astype(BF16)
+        to_across[c] = part(c, 3).astype(BF16)
         far_up(c).start()
-        to_across[d] = part(d, 0).astype(BF16)
+        to_across[d] = part(d, 3).astype(BF16)
         far_down(d).start()
         return carry
 
     lax.fori_loop(0, half, send_far, 0)
+    results = slots
     top = lax.broadcasted_iota(jnp.int32, (2 * CLEN, HS), 0) < CLEN
 
     def answers(p, carry):
         low, high = rows[0, 2 * p], rows[0, 2 * p + 1]
-        for h in range(keys.shape[2] // HS):
+        for h in range(heads):
             cols = pl.ds(h * HS, HS)
             k = jnp.concatenate([keys[low, :, cols], keys[high, :, cols]], 1)
             v = jnp.concatenate([values[low, :, cols], values[high, :, cols]], 1)
@@ -445,83 +470,75 @@
                 results[pl.ds(2 * p, 2), j, :, cols] = picked.reshape(2, CLEN, HS)
         return carry
 
-    lax.fori_loop(0, groups // 2, answers, 0, unroll=2)
-    start_results, wait_results = send_to_group(
-        groups, lambda g: results.at[g], fetched, send_sem, recv_sem
+    lax.fori_loop(0, groups // 2, answers, 0, unroll=4)
+    start, wait_answers = send_to_group(
+        groups, lambda g: results.at[g], answers_in, answer_send, answer_recv
     )
-    start_results()
-    local = pltpu.make_async_copy(results.at[me], fetched.at[me], local_sem)
-    local.start()
-    for pair in weight_loads[1:]:
-        for load in pair:
-            load.wait()
+    start()
+    local_answer = pltpu.make_async_copy(results.at[me], answers_in.at[me], local_sem.at[1])
+    local_answer.start()
 
     def send_near(c, carry):
         d = blocks - 1 - c
-        to_up[c] = part(c, 1).astype(BF16)
-        go_up(c).start()
-        to_down[d] = part(d, 2).astype(BF16)
-        go_down(d).start()
+        to_up[c] = part(c, 2).astype(BF16)
+        sum_up(c).start()
+        to_down[d] = part(d, 1).astype(BF16)
+        sum_down(d).start()
         return carry
 
     lax.fori_loop(half, blocks, send_near, 0)
 
     def send_joined(c, carry):
         d = blocks - 1 - c
-        mine = part(c, 1)
+        mine = part(c, 2)
         far_up(c).wait_recv()
         to_up[c] = (mine + from_far[c].astype(F32)).astype(BF16)
-        go_up(c).start()
-        mine = part(d, 2)
+        sum_up(c).start()
+        mine = part(d, 1)
         far_down(d).wait_recv()
         to_down[d] = (mine + from_far[d].astype(F32)).astype(BF16)
-        go_down(d).start()
+        sum_down(d).start()
         return carry
 
     lax.fori_loop(0, half, send_joined, 0)
 
-    def own(c, carry):
-        total[c] = part(c, 3)
-        return carry
-
-    lax.fori_loop(0, blocks, own, 0)
+    def keep_own(c, carry):
+        mine = part(c, 0)
+        key_acc[c] = mine[:, :width]
+        value_acc[c] = mine[:, width:]
+        return carry
+
+    lax.fori_loop(0, blocks, keep_own, 0)
+
+    def total(c, arrived):
+        other = arrived[c].astype(F32)
+        return key_acc[c] + other[:, :width], value_acc[c] + other[:, width:]
 
     def add_first(c, carry):
         d = blocks - 1 - c
-        go_up(c).wait_recv()
-        total[c] += before[c].astype(F32)
-        go_down(d).wait_recv()
-        total[d] += after[d].astype(F32)
+        sum_up(c).wait_recv()
+        key_acc[c], value_acc[c] = total(c, from_below)
+        sum_down(d).wait_recv()
+        key_acc[d], value_acc[d] = total(d, from_above)
         return carry
 
     lax.fori_loop(half, blocks, add_first, 0)
-    local.wait()
-    wait_results()
+    local_answer.wait()
+    wait_answers()
 
     def finish_span(t, carry):
         a, b = reads[0, t], reads[1, t]
-        attended[t] = (fetched[a, 0].astype(F32) + fetched[b, 0].astype(F32)).astype(BF16)
-        grad_q[t] = (fetched[a, 1].astype(F32) + fetched[b, 1].astype(F32)).astype(BF16)
+        for j, target in enumerate((query_in, grad_in)):
+            target[t] = (answers_in[a, j].astype(F32) + answers_in[b, j].astype(F32)).astype(BF16)
         return carry
 
     lax.fori_loop(0, spans, finish_span, 0)
-
-    def add_last(c, carry):
-        d = blocks - 1 - c
-        go_up(c).wait_recv()
-        grad_e[c] = (total[c] + before[c].astype(F32)).astype(BF16)
-        go_down(d).wait_recv()
-        grad_e[d] = (total[d] + after[d].astype(F32)).astype(BF16)
-        return carry
-
-    lax.fori_loop(0, half, add_last, 0)
-
-    def sent(c, carry):
-        go_up(c).wait_send()
-        go_down(c).wait_send()
-        return carry
-
-    lax.fori_loop(0, blocks, sent, 0)
+    out_copies = (
+        pltpu.make_async_copy(query_in, attended_out, out_sem.at[blocks]),
+        pltpu.make_async_copy(grad_in, grad_q_out, out_sem.at[blocks + 1]),
+    )
+    for copy in out_copies:
+        copy.start()
 
     def sent_far(c, carry):
         far_up(c).wait_send()
@@ -529,6 +546,36 @@
         return carry
 
     lax.fori_loop(0, half, sent_far, 0)
+    grad_e = own
+
+    def out_copy(c):
+        return pltpu.make_async_copy(grad_e.at[c], grad_e_out.at[c], out_sem.at[c])
+
+    def emit(c, arrived):
+        low, high = total(c, arrived)
+        grad_e[c, :, :width] = low.astype(BF16)
+        grad_e[c, :, width:] = high.astype(BF16)
+        out_copy(c).start()
+
+    def add_last(c, carry):
+        d = blocks - 1 - c
+        sum_up(c).wait_recv()
+        emit(c, from_below)
+        sum_down(d).wait_recv()
+        emit(d, from_above)
+        return carry
+
+    lax.fori_loop(0, half, add_last, 0)
+
+    def sums_sent(c, carry):
+        sum_up(c).wait_send()
+        sum_down(c).wait_send()
+        out_copy(c).wait()
+        return carry
+
+    lax.fori_loop(0, blocks, sums_sent, 0)
+    for copy in out_copies:
+        copy.wait()
 
 
 def finish_kernel(*refs):
@@ -569,14 +616,24 @@
     prob_shape = jax.ShapeDtypeStruct((half_pairs, heads, NLEN, 2 * CLEN), BF16)
 
     stat_rows = 16
-    keys, values, slots, probs, grad_s = pl.pallas_call(
-        functools.partial(project_kernel, groups),
-        out_shape=(block_shape, block_shape, slot_shape, prob_shape, prob_shape),
-        in_specs=[smem, smem, vmem, vmem, hbm, hbm, hbm],
-        out_specs=(vmem, vmem, hbm, vmem, vmem),
+    stat_shape = (groups, stat_rows, 2 * CLEN)
+    factor_shape = (groups, 2 * heads, 2 * CLEN)
+    span_shape = jax.ShapeDtypeStruct((spans, CLEN, width), BF16)
+    results = pl.pallas_call(
+        functools.partial(retro_kernel, groups),
+        out_shape=(span_shape, span_shape, jax.ShapeDtypeStruct(encoded.shape, BF16)),
+        in_specs=[smem, smem, hbm, hbm, hbm, hbm, hbm],
+        out_specs=(hbm, hbm, hbm),
         scratch_shapes=[
             pltpu.SMEM((groups,), jnp.int32),
             pltpu.SMEM((groups,), jnp.int32),
+            pltpu.SMEM((groups,), jnp.int32),
+            pltpu.SMEM((groups,), jnp.int32),
+            pltpu.SMEM((groups,), jnp.int32),
+            pltpu.SMEM((blocks,), jnp.int32),
+            pltpu.SMEM((blocks,), jnp.int32),
+            pltpu.VMEM(span_shape.shape, BF16),
+            pltpu.VMEM(span_shape.shape, BF16),
             pltpu.VMEM(slot_shape.shape, BF16),
             pltpu.VMEM(slot_shape.shape, BF16),
             pltpu.VMEM(encoded.shape, BF16),
@@ -585,16 +642,27 @@
             pltpu.VMEM(encoded.shape, BF16),
             pltpu.VMEM(key_parts.shape, BF16),
             pltpu.VMEM(key_parts.shape, BF16),
-            pltpu.VMEM((blocks, NLEN, width), F32),
-            pltpu.VMEM((blocks, NLEN, width), F32),
-            pltpu.VMEM((half_pairs, stat_rows, 2 * CLEN), F32),
-            pltpu.VMEM((groups, stat_rows, 2 * CLEN), F32),
-            pltpu.VMEM((spans, 2 * heads, 2 * CLEN), F32),
-            pltpu.VMEM((groups, 2 * heads, 2 * CLEN), F32),
-            pltpu.VMEM((groups, 2 * heads, 2 * CLEN), F32),
+            pltpu.VMEM(block_shape.shape, F32),
+            pltpu.VMEM(block_shape.shape, F32),
+            pltpu.VMEM(block_shape.shape, BF16),
+            pltpu.VMEM(block_shape.shape, BF16),
+            pltpu.VMEM(prob_shape.shape, BF16),
+            pltpu.VMEM(prob_shape.shape, BF16),
             pltpu.VMEM(prob_shape.shape, F32),
             pltpu.VMEM(prob_shape.shape, F32),
-            dma((9,)),
+            pltpu.VMEM((half_pairs,) + stat_shape[1:], F32),
+            pltpu.VMEM(stat_shape, F32),
+            pltpu.VMEM((spans,) + factor_shape[1:], F32),
+            pltpu.VMEM(factor_shape, F32),
+            pltpu.VMEM(factor_shape, F32),
+            pltpu.VMEM((NLEN, width), F32),
+            pltpu.VMEM((NLEN, width), F32),
+            pltpu.VMEM(slot_shape.shape, BF16),
+            pltpu.VMEM(slot_shape.shape, BF16),
+            pltpu.VMEM(encoded.shape, BF16),
+            pltpu.VMEM(encoded.shape, BF16),
+            pltpu.VMEM(encoded.shape, BF16),
+            dma((11,)),
             dma((3, blocks)),
             dma((3, blocks)),
             dma((groups,)),
@@ -604,64 +672,15 @@
             dma((groups,)),
             dma((groups,)),
             dma((groups,)),
-        ],
-        compiler_params=params(0),
-        name="project",
-    )(rows, reads, query_spans, grad_spans, encoded, key_parts, value_parts)
-
-    steps = 4
-    pairs = half_pairs // steps
-    whole = pl.BlockSpec(block_shape.shape, lambda i, rows: (0, 0, 0))
-    per_pair = pl.BlockSpec((pairs,) + prob_shape.shape[1:], lambda i, rows: (i, 0, 0, 0))
-    per_slot = pl.BlockSpec((2 * pairs,) + slot_shape.shape[1:], lambda i, rows: (i, 0, 0, 0))
-    grad_keys, grad_values = pl.pallas_call(
-        functools.partial(grads_kernel, pairs),
-        out_shape=(block_shape, block_shape),
-        grid_spec=pltpu.PrefetchScalarGridSpec(
-            num_scalar_prefetch=1,
-            grid=(steps,),
-            in_specs=[per_pair, per_pair, per_slot],
-            out_specs=(whole, whole),
-            scratch_shapes=[
-                pltpu.VMEM(block_shape.shape, F32),
-                pltpu.VMEM(block_shape.shape, F32),
-            ],
-        ),
-        compiler_params=params(),
-        name="grads",
-    )(send_rows.reshape(groups), probs, grad_s, slots)
-
-    results = pl.pallas_call(
-        functools.partial(reduce_kernel, groups),
-        out_shape=(
-            jax.ShapeDtypeStruct((spans, CLEN, width), BF16),
-            jax.ShapeDtypeStruct((spans, CLEN, width), BF16),
-            jax.ShapeDtypeStruct(encoded.shape, BF16),
-        ),
-        in_specs=[smem, smem, vmem, vmem, vmem, vmem, vmem, vmem, hbm, hbm],
-        out_specs=(vmem, vmem, vmem),
-        scratch_shapes=[
-            pltpu.VMEM(slot_shape.shape, BF16),
-            pltpu.VMEM(slot_shape.shape, BF16),
-            pltpu.VMEM(key_parts.shape, BF16),
-            pltpu.VMEM(key_parts.shape, BF16),
-            pltpu.VMEM(encoded.shape, BF16),
-            pltpu.VMEM(encoded.shape, BF16),
-            pltpu.VMEM(encoded.shape, BF16),
-            pltpu.VMEM(encoded.shape, BF16),
-            pltpu.VMEM(encoded.shape, BF16),
-            pltpu.VMEM(encoded.shape, BF16),
-            pltpu.VMEM(encoded.shape, F32),
-            dma((8,)),
             dma((3, blocks)),
             dma((3, blocks)),
             dma((groups,)),
             dma((groups,)),
-            dma,
+            dma((blocks + 2,)),
         ],
-        compiler_params=params(2),
-        name="reduce",
-    )(rows, reads, keys, values, probs, grad_s, grad_keys, grad_values, key_parts, value_parts)
+        compiler_params=params(0, 62),
+        name="retro",
+    )(rows, reads, query_spans, grad_spans, encoded, key_parts, value_parts)
     parts = 4
     slices = [
         pl.BlockSpec((r.shape[0] // parts,) + r.shape[1:], lambda i: (i, 0, 0)) for r in results

time: 197 us -> 179 us (0.909)
  Pallas kernels: 196 us -> 178 us
    pallas_call x3 -> x1, Pallas kernels: 192 us -> 174 us  [body(): pl.pallas_call(functools.partial(retro_kernel, groups), out_shape=(span_s...]
where the time goes in v3:
time: 179 us
  Pallas kernels  178 us (99%)
    pallas_call x1, Pallas kernels, body(): pl.pallas_call(functools.partial(retro_kernel, groups), out_shape=(span_s...  174 us
    pallas_call x1, Pallas kernels, body(): pl.pallas_call(finish_kernel, out_shape=tuple((jax.ShapeDtypeStruct(r.sha...  4.23 us

profile of v3, /device:TPU:16, one launch (start us, length us, event | category | flops | bytes accessed | tf_op | source)
XLA Modules:
  0.0 178.6 jit_solution(12345249570972626166)
XLA Ops:
  0.6 173.7 %retro.1 = (bf16[8,64,512]{2,1,0:T(8,128)(2,1)}, bf16[8,64,512]{2,1,0:T(8,128)(2,1)}, bf16[8,128,1024]{2,1,0:T(8,128)(2,1)}) custom-call(s32[1,32]{1,0:T(1,128)} %bitcast.13, s32[2,8]{1,0:T(2,128)} %bitcast.12, bf16[8,64,512]{2,1,0:T(8,128)(2,1)} %bitcast.10, bf16[8,64,512]{2,1,0:T(8,128)(2,1)} %bitcast.11, bf16[8,128,1024]{2,1,0:T(8,128)(2,1)} %encoded.1, ...), custom_call_target="tpu_custom_call" | custom-call | tf_op jit(solution)/shard_map/retro/pallas_call | solution.py:622
  174.3 4.2 %finish.1 = (bf16[8,64,512]{2,1,0:T(8,128)(2,1)}, bf16[8,64,512]{2,1,0:T(8,128)(2,1)}, bf16[8,128,1024]{2,1,0:T(8,128)(2,1)}) custom-call(bf16[8,64,512]{2,1,0:T(8,128)(2,1)} %get-tuple-element.9.refs_0_, bf16[8,64,512]{2,1,0:T(8,128)(2,1)} %get-tuple-element.10.refs_1_, bf16[8,128,1024]{2,1,0:T(8,128)(2,1)} %get-tuple-element.11.refs_2_), custom_call_target="tpu_custom_call" | custom-call | tf_op jit(solution)/shard_map/finish/pallas_call | solution.py:688

commit v4 on v3

--- a/solution.py
+++ b/solution.py
@@ -64,18 +64,17 @@
             device_id_type=MESH,
         )
 
-    def start():
-        lax.fori_loop(1, groups, lambda k, c: (copy_to(k).start(), c)[1], 0)
-
-    def wait():
-        def one(k, carry):
-            copy_from(k).wait_recv()
-            copy_to(k).wait_send()
-            return carry
-
-        lax.fori_loop(1, groups, one, 0)
-
-    return start, wait
+    def arrive():
+        lax.fori_loop(1, groups, lambda k, c: (copy_from(k).wait_recv(), c)[1], 0)
+
+    def leave():
+        lax.fori_loop(1, groups, lambda k, c: (copy_to(k).wait_send(), c)[1], 0)
+
+    return copy_to, arrive, leave
+
+
+def start_all(groups, copy_to):
+    lax.fori_loop(1, groups, lambda k, c: (copy_to(k).start(), c)[1], 0)
 
 
 def diagonal(slots, first, which, cols):
@@ -95,15 +94,15 @@
 
 def retro_kernel(
     groups, rows, reads, queries, grads, encoded, key_weight, value_weight,
-    attended_out, grad_q_out, grad_e_out,
+    attended, grad_q, grad_e,
     source, live, rank, order, keep, final, filled,
     query_in, grad_in, outgoing, slots, own, before, after, far, key_w, value_w,
-    key_acc, value_acc, keys, values, probs, grad_s, weights, grad_p,
-    stats, fetched, combined, back, landed, key_run, value_run, value_sums,
+    totals, keys, values, probs, grad_s, grad_p,
+    peaks, stats, fetched, combined, back, landed, key_run, value_run, value_sums,
     answers_in, from_far, from_below, from_above,
     load_sem, ring_send, ring_recv, send_sem, recv_sem, local_sem,
     stat_send, stat_recv, back_send, back_recv,
-    sum_send, sum_recv, answer_send, answer_recv, out_sem,
+    sum_send, sum_recv, answer_send, answer_recv,
 ):
     me = group_index()
     z = lax.axis_index("mp")
@@ -112,6 +111,7 @@
     across = lax.rem(z + 2, ring)
     blocks = encoded.shape[0]
     half = blocks // 2
+    key_acc, value_acc, weights = totals.at[0], totals.at[1], totals
 
     barrier = pltpu.get_barrier_semaphore()
     pl.semaphore_signal(barrier, inc=1, device_id={"mp": up}, device_id_type=MESH)
@@ -186,10 +186,10 @@
     for load in inputs:
         load.wait()
     lax.fori_loop(0, groups, fill, 0)
-    start_slots, wait_slots = send_to_group(
+    slot_to, slots_arrive, slots_leave = send_to_group(
         groups, lambda g: outgoing.at[g], slots, send_sem, recv_sem
     )
-    start_slots()
+    start_all(groups, slot_to)
     local = pltpu.make_async_copy(outgoing.at[me], slots.at[me], local_sem.at[0])
     local.start()
 
@@ -283,7 +283,8 @@
 
     lax.fori_loop(half, blocks, rest, 0)
 
-    wait_slots()
+    slots_arrive()
+    slots_leave()
     local.wait()
 
     def last(c, carry):
@@ -298,64 +299,99 @@
 
     heads = keys.shape[2] // HS
 
-    def score(p, carry):
+    def score(p):
         for h in range(heads):
             k, v, q, g = pair_operands(rows, p, keys, values, slots, 2 * p, h)
             scores = lax.dot_general(k, q, LAST, preferred_element_type=F32) * SCALE
             gp = lax.dot_general(v, g, LAST, preferred_element_type=F32)
             peak = jnp.max(scores, 0, keepdims=True)
             w = jnp.exp(scores - peak)
-            stats[p, h : h + 1] = peak
-            stats[p, heads + h : heads + h + 1] = jnp.sum(w, 0, keepdims=True)
-            stats[p, 2 * heads + h : 2 * heads + h + 1] = jnp.sum(w * gp, 0, keepdims=True)
-            weights[p, h] = w
+            total = jnp.sum(w, 0, keepdims=True)
+            peaks[p, h : h + 1] = peak
+            stats[p, h : h + 1] = peak + jnp.log(total)
+            stats[p, heads + h : heads + h + 1] = jnp.sum(w * gp, 0, keepdims=True) / total
+            weights[p // blocks, p % blocks, :, h * HS : (h + 1) * HS] = w
             grad_p[p, h] = gp
-        stats[p, 3 * heads :] = jnp.zeros((stats.shape[1] - 3 * heads, 2 * CLEN), F32)
-        return carry
-
-    lax.fori_loop(0, groups // 2, score, 0, unroll=4)
-
-    start, wait = send_to_group(
+
+    stat_to, stats_arrive, stats_leave = send_to_group(
         groups, lambda g: stats.at[g // 2], fetched, stat_send, stat_recv
     )
-    start()
-    local = pltpu.make_async_copy(stats.at[me // 2], fetched.at[me], local_sem.at[2])
-    local.start()
-    local.wait()
-    wait()
+    local_stat = pltpu.make_async_copy(stats.at[me // 2], fetched.at[me], local_sem.at[2])
+    together = 4
+    chunks = groups // 2 // together
+
+    def score_some(j, carry):
+        first = together * lax.rem(me // (2 * together) + j, chunks)
+        for u in range(together):
+            score(first + u)
+        for u in range(2 * together):
+            k = lax.rem(2 * first + u + groups - me, groups)
+
+            @pl.when(k > 0)
+            def _():
+                stat_to(k).start()
+
+            @pl.when(k == 0)
+            def _():
+                local_stat.start()
+
+        return carry
+
+    lax.fori_loop(0, chunks, score_some, 0)
+
+    def sent(c, carry):
+        go_up(c).wait_send()
+        go_down(c).wait_send()
+        return carry
+
+    lax.fori_loop(0, blocks, sent, 0)
+
+    def passed(c, carry):
+        pass_up(c).wait_send()
+        pass_down(blocks - 1 - c).wait_send()
+        return carry
+
+    lax.fori_loop(0, half, passed, 0)
+    local_stat.wait()
+    stats_arrive()
 
     def combine(t, carry):
         a = fetched[reads[0, t]]
         b = fetched[reads[1, t]]
         overall = jnp.maximum(a[:heads], b[:heads])
         fa, fb = jnp.exp(a[:heads] - overall), jnp.exp(b[:heads] - overall)
-        total = fa * a[heads : 2 * heads] + fb * b[heads : 2 * heads]
-        grad = fa * a[2 * heads : 3 * heads] + fb * b[2 * heads : 3 * heads]
+        total = fa + fb
         combined[t, :heads] = overall + jnp.log(total)
-        combined[t, heads:] = grad / total
+        combined[t, heads:] = (fa * a[heads:] + fb * b[heads:]) / total
         return carry
 
     lax.fori_loop(0, spans, combine, 0, unroll=8)
-
-    def answer(o, carry):
+    back_to, backs_arrive, backs_leave = send_to_group(
+        groups, lambda g: back.at[g], landed, back_send, back_recv
+    )
+
+    def answer(o):
         mine = combined[source[o]]
         back[o] = jnp.where(live[o] > 0, mine, jnp.zeros_like(mine))
-        return carry
-
-    lax.fori_loop(0, groups, answer, 0, unroll=8)
-    start, wait = send_to_group(groups, lambda g: back.at[g], landed, back_send, back_recv)
-    start()
+
+    def answer_to(k, carry):
+        answer(lax.rem(me + k, groups))
+        back_to(k).start()
+        return carry
+
+    lax.fori_loop(1, groups, answer_to, 0)
+    answer(me)
     local = pltpu.make_async_copy(back.at[me], landed.at[me], local_sem.at[3])
     local.start()
     local.wait()
-    wait()
+    backs_arrive()
     left = lax.broadcasted_iota(jnp.int32, landed.shape[1:], 1) < CLEN
 
     def normalise(p, carry):
         both = jnp.where(left, landed[2 * p], landed[2 * p + 1])
         for h in range(heads):
-            factor = jnp.exp(stats[p, h : h + 1] - both[h : h + 1])
-            pr = weights[p, h] * factor
+            factor = jnp.exp(peaks[p, h : h + 1] - both[h : h + 1])
+            pr = weights[p // blocks, p % blocks, :, h * HS : (h + 1) * HS] * factor
             probs[p, h] = pr.astype(BF16)
             grad_s[p, h] = (pr * (grad_p[p, h] - both[heads + h : heads + h + 1])).astype(BF16)
         return carry
@@ -389,32 +425,16 @@
             value_sums[i, :, :, cols] = v.astype(BF16).reshape(2, CLEN, HS)
         return carry
 
-    lax.fori_loop(0, groups, accumulate, 0, unroll=4)
+    lax.fori_loop(0, groups, accumulate, 0, unroll=8)
     width = keys.shape[2]
 
-    def gather(n, carry):
+    def gather(n):
         for j, sums in enumerate((outgoing, value_sums)):
             block = sums[final[n]].reshape(NLEN, width)
             far[n, :, j * width : (j + 1) * width] = jnp.where(
                 filled[n] > 0, block, jnp.zeros_like(block)
             )
-        return carry
-
-    lax.fori_loop(0, blocks, gather, 0)
-
-    def sent(c, carry):
-        go_up(c).wait_send()
-        go_down(c).wait_send()
-        return carry
-
-    lax.fori_loop(0, blocks, sent, 0)
-
-    def passed(c, carry):
-        pass_up(c).wait_send()
-        pass_down(blocks - 1 - c).wait_send()
-        return carry
-
-    lax.fori_loop(0, half, passed, 0)
+
 
     def part(c, i):
         return lax.dot_general(
@@ -447,8 +467,10 @@
 
     def send_far(c, carry):
         d = blocks - 1 - c
+        gather(c)
         to_across[c] = part(c, 3).astype(BF16)
         far_up(c).start()
+        gather(d)
         to_across[d] = part(d, 3).astype(BF16)
         far_down(d).start()
         return carry
@@ -471,10 +493,10 @@
         return carry
 
     lax.fori_loop(0, groups // 2, answers, 0, unroll=4)
-    start, wait_answers = send_to_group(
+    answer_copy, answers_arrive, answers_leave = send_to_group(
         groups, lambda g: results.at[g], answers_in, answer_send, answer_recv
     )
-    start()
+    start_all(groups, answer_copy)
     local_answer = pltpu.make_async_copy(results.at[me], answers_in.at[me], local_sem.at[1])
     local_answer.start()
 
@@ -524,38 +546,29 @@
 
     lax.fori_loop(half, blocks, add_first, 0)
     local_answer.wait()
-    wait_answers()
+    answers_arrive()
+    answers_leave()
+    stats_leave()
+    backs_leave()
 
     def finish_span(t, carry):
         a, b = reads[0, t], reads[1, t]
-        for j, target in enumerate((query_in, grad_in)):
+        for j, target in enumerate((attended, grad_q)):
             target[t] = (answers_in[a, j].astype(F32) + answers_in[b, j].astype(F32)).astype(BF16)
         return carry
 
     lax.fori_loop(0, spans, finish_span, 0)
-    out_copies = (
-        pltpu.make_async_copy(query_in, attended_out, out_sem.at[blocks]),
-        pltpu.make_async_copy(grad_in, grad_q_out, out_sem.at[blocks + 1]),
-    )
-    for copy in out_copies:
-        copy.start()
-
     def sent_far(c, carry):
         far_up(c).wait_send()
         far_down(blocks - 1 - c).wait_send()
         return carry
 
     lax.fori_loop(0, half, sent_far, 0)
-    grad_e = own
-
-    def out_copy(c):
-        return pltpu.make_async_copy(grad_e.at[c], grad_e_out.at[c], out_sem.at[c])
 
     def emit(c, arrived):
         low, high = total(c, arrived)
         grad_e[c, :, :width] = low.astype(BF16)
         grad_e[c, :, width:] = high.astype(BF16)
-        out_copy(c).start()
 
     def add_last(c, carry):
         d = blocks - 1 - c
@@ -570,18 +583,9 @@
     def sums_sent(c, carry):
         sum_up(c).wait_send()
         sum_down(c).wait_send()
-        out_copy(c).wait()
         return carry
 
     lax.fori_loop(0, blocks, sums_sent, 0)
-    for copy in out_copies:
-        copy.wait()
-
-
-def finish_kernel(*refs):
-    count = len(refs) // 2
-    for source, target in zip(refs[:count], refs[count:]):
-        target[...] = source[...]
 
 
 def params(collective_id=None, mib=56):
@@ -615,15 +619,18 @@
     slot_shape = jax.ShapeDtypeStruct((groups, 2, CLEN, width), BF16)
     prob_shape = jax.ShapeDtypeStruct((half_pairs, heads, NLEN, 2 * CLEN), BF16)
 
-    stat_rows = 16
-    stat_shape = (groups, stat_rows, 2 * CLEN)
+    stat_shape = (groups, 2 * heads, 2 * CLEN)
     factor_shape = (groups, 2 * heads, 2 * CLEN)
     span_shape = jax.ShapeDtypeStruct((spans, CLEN, width), BF16)
-    results = pl.pallas_call(
+    attended, grad_q, grad_e = pl.pallas_call(
         functools.partial(retro_kernel, groups),
-        out_shape=(span_shape, span_shape, jax.ShapeDtypeStruct(encoded.shape, BF16)),
+        out_shape=(
+            pltpu.VMEM(span_shape.shape, BF16),
+            pltpu.VMEM(span_shape.shape, BF16),
+            pltpu.VMEM(encoded.shape, BF16),
+        ),
         in_specs=[smem, smem, hbm, hbm, hbm, hbm, hbm],
-        out_specs=(hbm, hbm, hbm),
+        out_specs=(vmem, vmem, vmem),
         scratch_shapes=[
             pltpu.SMEM((groups,), jnp.int32),
             pltpu.SMEM((groups,), jnp.int32),
@@ -642,14 +649,13 @@
             pltpu.VMEM(encoded.shape, BF16),
             pltpu.VMEM(key_parts.shape, BF16),
             pltpu.VMEM(key_parts.shape, BF16),
-            pltpu.VMEM(block_shape.shape, F32),
-            pltpu.VMEM(block_shape.shape, F32),
+            pltpu.VMEM((2,) + block_shape.shape, F32),
             pltpu.VMEM(block_shape.shape, BF16),
             pltpu.VMEM(block_shape.shape, BF16),
             pltpu.VMEM(prob_shape.shape, BF16),
             pltpu.VMEM(prob_shape.shape, BF16),
             pltpu.VMEM(prob_shape.shape, F32),
-            pltpu.VMEM(prob_shape.shape, F32),
+            pltpu.VMEM((half_pairs,) + stat_shape[1:], F32),
             pltpu.VMEM((half_pairs,) + stat_shape[1:], F32),
             pltpu.VMEM(stat_shape, F32),
             pltpu.VMEM((spans,) + factor_shape[1:], F32),
@@ -676,24 +682,10 @@
             dma((3, blocks)),
             dma((groups,)),
             dma((groups,)),
-            dma((blocks + 2,)),
         ],
-        compiler_params=params(0, 62),
+        compiler_params=params(0, 58),
         name="retro",
     )(rows, reads, query_spans, grad_spans, encoded, key_parts, value_parts)
-    parts = 4
-    slices = [
-        pl.BlockSpec((r.shape[0] // parts,) + r.shape[1:], lambda i: (i, 0, 0)) for r in results
-    ]
-    attended, grad_q, grad_e = pl.pallas_call(
-        finish_kernel,
-        out_shape=tuple(jax.ShapeDtypeStruct(r.shape, r.dtype) for r in results),
-        grid=(parts,),
-        in_specs=slices,
-        out_specs=tuple(slices),
-        compiler_params=params(),
-        name="finish",
-    )(*results)
     return (attended.reshape(queries.shape), grad_q.reshape(queries.shape), grad_e)
 
 

time: 179 us -> 176 us (0.983)
  Pallas kernels: 178 us -> 172 us
  local copies, waits for them, and re-layouts: 0 us -> 2.91 us
    pallas_call x2 -> x1, Pallas kernels: 178 us -> 172 us  [body(): pl.pallas_call(functools.partial(retro_kernel, groups), out_shape=(pltpu....]
    unnamed x0 -> x3, local copies, waits for them, and re-layouts: none -> 2.91 us
where the time goes in v4:
time: 176 us; the launch traced here: 175 us
  Pallas kernels  172 us (98%)
  local copies, waits for them, and re-layouts  2.91 us (2%)
    pallas_call x1, Pallas kernels, body(): pl.pallas_call(functools.partial(retro_kernel, groups), out_shape=(pltpu....  172 us

profile of v4, /device:TPU:16, one launch (start us, length us, event | category | flops | bytes accessed | tf_op | source)
XLA Modules:
  0.0 175.1 jit_solution(15087099638409434691)
XLA Ops:
  0.6 171.5 %retro.1 = (bf16[8,64,512]{2,1,0:T(8,128)(2,1)S(1)}, bf16[8,64,512]{2,1,0:T(8,128)(2,1)S(1)}, bf16[8,128,1024]{2,1,0:T(8,128)(2,1)S(1)}) custom-call(s32[1,32]{1,0:T(1,128)} %bitcast.15, s32[2,8]{1,0:T(2,128)} %bitcast.14, bf16[8,64,512]{2,1,0:T(8,128)(2,1)} %bitcast.12, bf16[8,64,512]{2,1,0:T(8,128)(2,1)} %bitcast.13, bf16[8,128,1024]{2,1,0:T(8,128)(2,1)} %encoded.1, ...), custom_call_target="tpu_custom_call" | custom-call | tf_op jit(solution)/shard_map/retro/pallas_call | solution.py:625
  172.2 0.8 copy.13
  172.9 0.8 copy.14
  173.7 1.3 copy.15

commit v5 on v4

--- a/solution.py
+++ b/solution.py
@@ -47,28 +47,28 @@
         return pltpu.make_async_remote_copy(
             src_ref=source(peer),
             dst_ref=target.at[me],
-            send_sem=send_sem.at[k],
-            recv_sem=recv_sem.at[k],
+            send_sem=send_sem,
+            recv_sem=recv_sem,
             device_id=peer_id(peer),
             device_id_type=MESH,
         )
 
-    def copy_from(k):
-        peer = lax.rem(me + groups - k, groups)
+    def everything():
+        others = target.at[pl.ds(0, groups - 1)]
         return pltpu.make_async_remote_copy(
-            src_ref=source(peer),
-            dst_ref=target.at[peer],
-            send_sem=send_sem.at[k],
-            recv_sem=recv_sem.at[k],
-            device_id=peer_id(peer),
+            src_ref=others,
+            dst_ref=others,
+            send_sem=send_sem,
+            recv_sem=recv_sem,
+            device_id=peer_id(lax.rem(me + 1, groups)),
             device_id_type=MESH,
         )
 
     def arrive():
-        lax.fori_loop(1, groups, lambda k, c: (copy_from(k).wait_recv(), c)[1], 0)
+        everything().wait_recv()
 
     def leave():
-        lax.fori_loop(1, groups, lambda k, c: (copy_to(k).wait_send(), c)[1], 0)
+        everything().wait_send()
 
     return copy_to, arrive, leave
 
@@ -140,7 +140,7 @@
         return pltpu.make_async_remote_copy(
             src_ref=source.at[block],
             dst_ref=target.at[block],
-            send_sem=ring_send.at[lane, block],
+            send_sem=ring_send.at[lane],
             recv_sem=ring_recv.at[lane, block],
             device_id={"mp": to},
             device_id_type=MESH,
@@ -339,19 +339,19 @@
 
     lax.fori_loop(0, chunks, score_some, 0)
 
-    def sent(c, carry):
-        go_up(c).wait_send()
-        go_down(c).wait_send()
-        return carry
-
-    lax.fori_loop(0, blocks, sent, 0)
-
-    def passed(c, carry):
-        pass_up(c).wait_send()
-        pass_down(blocks - 1 - c).wait_send()
-        return carry
-
-    lax.fori_loop(0, half, passed, 0)
+    def all_sent(lane, source, sem):
+        pltpu.make_async_remote_copy(
+            src_ref=source,
+            dst_ref=source,
+            send_sem=sem.at[lane],
+            recv_sem=ring_recv.at[0, 0],
+            device_id={"mp": up},
+            device_id_type=MESH,
+        ).wait_send()
+
+    for lane in range(3):
+        all_sent(lane, far, ring_send)
+
     local_stat.wait()
     stats_arrive()
 
@@ -445,7 +445,7 @@
         return pltpu.make_async_remote_copy(
             src_ref=source.at[block],
             dst_ref=target.at[block],
-            send_sem=sum_send.at[lane, block],
+            send_sem=sum_send.at[lane],
             recv_sem=sum_recv.at[lane, block],
             device_id={"mp": to},
             device_id_type=MESH,
@@ -558,13 +558,6 @@
         return carry
 
     lax.fori_loop(0, spans, finish_span, 0)
-    def sent_far(c, carry):
-        far_up(c).wait_send()
-        far_down(blocks - 1 - c).wait_send()
-        return carry
-
-    lax.fori_loop(0, half, sent_far, 0)
-
     def emit(c, arrived):
         low, high = total(c, arrived)
         grad_e[c, :, :width] = low.astype(BF16)
@@ -580,12 +573,8 @@
 
     lax.fori_loop(0, half, add_last, 0)
 
-    def sums_sent(c, carry):
-        sum_up(c).wait_send()
-        sum_down(c).wait_send()
-        return carry
-
-    lax.fori_loop(0, blocks, sums_sent, 0)
+    for lane in range(3):
+        all_sent(lane, far, sum_send)
 
 
 def params(collective_id=None, mib=56):
@@ -669,19 +658,19 @@
             pltpu.VMEM(encoded.shape, BF16),
             pltpu.VMEM(encoded.shape, BF16),
             dma((11,)),
+            dma((3,)),
             dma((3, blocks)),
+            dma,
+            dma,
+            dma((4,)),
+            dma,
+            dma,
+            dma,
+            dma,
+            dma((3,)),
             dma((3, blocks)),
-            dma((groups,)),
-            dma((groups,)),
-            dma((4,)),
-            dma((groups,)),
-            dma((groups,)),
-            dma((groups,)),
-            dma((groups,)),
-            dma((3, blocks)),
-            dma((3, blocks)),
-            dma((groups,)),
-            dma((groups,)),
+            dma,
+            dma,
         ],
         compiler_params=params(0, 58),
         name="retro",

time: 176 us -> 173 us (0.983)
  Pallas kernels: 172 us -> 169 us
    pallas_call x1, Pallas kernels: 172 us -> 169 us  [body(): pl.pallas_call(functools.partial(retro_kernel, groups), out_shape=(pltpu....]
where the time goes in v5:
time: 173 us
  Pallas kernels  169 us (98%)
  local copies, waits for them, and re-layouts  2.91 us (2%)
    pallas_call x1, Pallas kernels, body(): pl.pallas_call(functools.partial(retro_kernel, groups), out_shape=(pltpu....  169 us

profile of v5, /device:TPU:16, one launch (start us, length us, event | category | flops | bytes accessed | tf_op | source)
XLA Modules:
  0.0 172.8 jit_solution(13364736061415289683)
XLA Ops:
  0.6 169.3 %retro.1 = (bf16[8,64,512]{2,1,0:T(8,128)(2,1)S(1)}, bf16[8,64,512]{2,1,0:T(8,128)(2,1)S(1)}, bf16[8,128,1024]{2,1,0:T(8,128)(2,1)S(1)}) custom-call(s32[1,32]{1,0:T(1,128)} %bitcast.15, s32[2,8]{1,0:T(2,128)} %bitcast.14, bf16[8,64,512]{2,1,0:T(8,128)(2,1)} %bitcast.12, bf16[8,64,512]{2,1,0:T(8,128)(2,1)} %bitcast.13, bf16[8,128,1024]{2,1,0:T(8,128)(2,1)} %encoded.1, ...), custom_call_target="tpu_custom_call" | custom-call | tf_op jit(solution)/shard_map/retro/pallas_call | solution.py:614
  169.9 0.8 copy.13
  170.7 0.8 copy.14
  171.5 1.3 copy.15

commit v6 on v5

--- a/solution.py
+++ b/solution.py
@@ -99,16 +99,21 @@
     query_in, grad_in, outgoing, slots, own, before, after, far, key_w, value_w,
     totals, keys, values, probs, grad_s, grad_p,
     peaks, stats, fetched, combined, back, landed, key_run, value_run, value_sums,
-    answers_in, from_far, from_below, from_above,
+    outs_in, grad_qs_in, cross_grads, pair_sums, cross_w,
     load_sem, ring_send, ring_recv, send_sem, recv_sem, local_sem,
     stat_send, stat_recv, back_send, back_recv,
-    sum_send, sum_recv, answer_send, answer_recv,
+    sum_send, sum_recv, answer_send, answer_recv, grad_q_send, grad_q_recv, weight_send, weight_recv,
 ):
     me = group_index()
     z = lax.axis_index("mp")
     ring = lax.axis_size("mp")
     up, down = lax.rem(z + 1, ring), lax.rem(z + ring - 1, ring)
     across = lax.rem(z + 2, ring)
+    cross = ring - 1 - z
+    partner = z + 1 - 2 * lax.rem(z, 2)
+    pair_slot = 2 - lax.rem(z, 2)
+    phase, dp = lax.axis_index("phase"), lax.axis_index("dp")
+    in_phase = lax.axis_size("dp")
     blocks = encoded.shape[0]
     half = blocks // 2
     key_acc, value_acc, weights = totals.at[0], totals.at[1], totals
@@ -160,6 +165,56 @@
 
     pl.semaphore_wait(barrier, groups - 1 + 2)
 
+    cross_pair = cross + 1 - 2 * lax.rem(cross, 2)
+    their_part = cross * (1 - phase) + cross_pair * phase
+    piece_rows = pl.ds(pl.multiple_of(dp * CLEN, CLEN), CLEN)
+
+    def piece_copy(j, weight):
+        return pltpu.make_async_remote_copy(
+            src_ref=weight.at[their_part, piece_rows],
+            dst_ref=cross_w.at[me, j],
+            send_sem=weight_send.at[0],
+            recv_sem=weight_recv.at[0],
+            device_id={"mp": cross},
+            device_id_type=MESH,
+        )
+
+    def weight_copy(stage, block, to):
+        return pltpu.make_async_remote_copy(
+            src_ref=cross_w.at[block],
+            dst_ref=cross_w.at[block],
+            send_sem=weight_send.at[stage],
+            recv_sem=weight_recv.at[stage],
+            device_id=to,
+            device_id_type=MESH,
+        )
+
+    side = round(in_phase**0.5)
+    x, y = lax.rem(dp, side), dp // side
+
+    def first_line(k):
+        return lax.rem(y + k * phase, side) * side + lax.rem(x + k * (1 - phase), side)
+
+    def second_line(k):
+        return lax.rem(y + k * (1 - phase), side) * side + lax.rem(x + k * phase, side)
+
+    def spread_first(k, carry):
+        weight_copy(1, me, {"dp": first_line(k)}).start()
+        return carry
+
+    def spread_second(i, carry):
+        piece = phase * in_phase + first_line(i // (side - 1))
+        to = second_line(1 + lax.rem(i, side - 1))
+        weight_copy(2, piece, {"dp": to}).start()
+        return carry
+
+    pieces = weight_copy(0, me, {"mp": cross})
+    firsts = weight_copy(1, pl.ds(0, side - 1), {"dp": first_line(1)})
+    seconds = weight_copy(2, pl.ds(0, side * (side - 1)), {"dp": second_line(1)})
+    halves = weight_copy(3, pl.ds(phase * in_phase, in_phase), {"phase": 1 - phase})
+    piece_copy(0, key_weight).start()
+    piece_copy(1, value_weight).start()
+
     def send_own(c, carry):
         go_up(c).start()
         go_down(blocks - 1 - c).start()
@@ -186,6 +241,8 @@
     for load in inputs:
         load.wait()
     lax.fori_loop(0, groups, fill, 0)
+    pieces.wait_recv()
+    lax.fori_loop(1, side, spread_first, 0)
     slot_to, slots_arrive, slots_leave = send_to_group(
         groups, lambda g: outgoing.at[g], slots, send_sem, recv_sem
     )
@@ -229,6 +286,8 @@
     lax.fori_loop(0, groups, invert, 0)
     lax.fori_loop(0, groups, follow, 0)
     lax.fori_loop(0, blocks, close, 0)
+    firsts.wait_recv()
+    lax.fori_loop(0, side * (side - 1), spread_second, 0)
 
     def project(block, i):
         return (
@@ -283,9 +342,6 @@
 
     lax.fori_loop(half, blocks, rest, 0)
 
-    slots_arrive()
-    slots_leave()
-    local.wait()
 
     def last(c, carry):
         d = blocks - 1 - c
@@ -297,7 +353,13 @@
 
     lax.fori_loop(0, half, last, 0)
 
-    heads = keys.shape[2] // HS
+    slots_arrive()
+    slots_leave()
+    local.wait()
+    seconds.wait_recv()
+    halves.start()
+    width = keys.shape[2]
+    heads = width // HS
 
     def score(p):
         for h in range(heads):
@@ -398,6 +460,35 @@
 
     lax.fori_loop(0, groups // 2, normalise, 0, unroll=2)
 
+    top = lax.broadcasted_iota(jnp.int32, (2 * CLEN, HS), 0) < CLEN
+
+    def slot_view(buffer, g):
+        start = pl.multiple_of(lax.rem(g // 2, 2) * CLEN, CLEN)
+        column = pl.multiple_of(lax.rem(g, 2) * width, width)
+        return buffer.at[g // 4, pl.ds(start, CLEN), pl.ds(column, width)]
+
+    def answer_all(lefts, rights, scale, buffer):
+        def one(p, carry):
+            low, high = rows[0, 2 * p], rows[0, 2 * p + 1]
+            start = pl.multiple_of(lax.rem(p, 2) * CLEN, CLEN)
+            for h in range(heads):
+                cols = pl.ds(h * HS, HS)
+                right = jnp.concatenate([rights[low, :, cols], rights[high, :, cols]], 1)
+                both = lax.dot_general(lefts[p, h], right, FIRST, preferred_element_type=F32)
+                picked = (jnp.where(top, both[:, :HS], both[:, HS:]) * scale).astype(BF16)
+                buffer[p // 2, pl.ds(start, CLEN), h * HS : (h + 1) * HS] = picked[:CLEN]
+                buffer[p // 2, pl.ds(start, CLEN), width + h * HS : width + (h + 1) * HS] = picked[CLEN:]
+            return carry
+
+        lax.fori_loop(0, groups // 2, one, 0, unroll=4)
+
+    answer_all(probs, values, 1.0, before)
+    out_to, outs_arrive, outs_leave = send_to_group(
+        groups, lambda g: slot_view(before, g), outs_in, answer_send, answer_recv
+    )
+    start_all(groups, out_to)
+    local_out = pltpu.make_async_copy(slot_view(before, me), outs_in.at[me], local_sem.at[1])
+    local_out.start()
     half_lane = lax.broadcasted_iota(jnp.int32, (NLEN, 2 * CLEN), 1) // CLEN
     key_run[...] = jnp.zeros_like(key_run)
     value_run[...] = jnp.zeros_like(value_run)
@@ -426,8 +517,6 @@
         return carry
 
     lax.fori_loop(0, groups, accumulate, 0, unroll=8)
-    width = keys.shape[2]
-
     def gather(n):
         for j, sums in enumerate((outgoing, value_sums)):
             block = sums[final[n]].reshape(NLEN, width)
@@ -436,10 +525,19 @@
             )
 
 
-    def part(c, i):
+    def own_part(c, i):
         return lax.dot_general(
             far[c, :, :width], key_w[i], LAST, preferred_element_type=F32
         ) + lax.dot_general(far[c, :, width:], value_w[i], LAST, preferred_element_type=F32)
+
+    def cross_part(c, i):
+        some = pl.ds(i * in_phase, in_phase)
+        shape = (in_phase * CLEN, width)
+        return lax.dot_general(
+            cross_grads[c, :, :width], cross_w[some, 0].reshape(shape), LAST, preferred_element_type=F32
+        ) + lax.dot_general(
+            cross_grads[c, :, width:], cross_w[some, 1].reshape(shape), LAST, preferred_element_type=F32
+        )
 
     def sum_copy(lane, source, target, block, to):
         return pltpu.make_async_remote_copy(
@@ -451,130 +549,69 @@
             device_id_type=MESH,
         )
 
-    to_across, to_up, to_down = own, before, after
-
-    def far_up(c):
-        return sum_copy(2, to_across, from_far, c, up)
-
-    def far_down(c):
-        return sum_copy(2, to_across, from_far, c, down)
-
-    def sum_up(c):
-        return sum_copy(0, to_up, from_below, c, up)
-
-    def sum_down(c):
-        return sum_copy(1, to_down, from_above, c, down)
-
-    def send_far(c, carry):
-        d = blocks - 1 - c
+    to_pair = own
+
+    def cross_copy(c):
+        return sum_copy(0, far, cross_grads, c, cross)
+
+    def pair_copy(c):
+        return sum_copy(1, to_pair, pair_sums, c, partner)
+
+    def send_cross(c, carry):
         gather(c)
-        to_across[c] = part(c, 3).astype(BF16)
-        far_up(c).start()
-        gather(d)
-        to_across[d] = part(d, 3).astype(BF16)
-        far_down(d).start()
-        return carry
-
-    lax.fori_loop(0, half, send_far, 0)
-    results = slots
-    top = lax.broadcasted_iota(jnp.int32, (2 * CLEN, HS), 0) < CLEN
-
-    def answers(p, carry):
-        low, high = rows[0, 2 * p], rows[0, 2 * p + 1]
-        for h in range(heads):
-            cols = pl.ds(h * HS, HS)
-            k = jnp.concatenate([keys[low, :, cols], keys[high, :, cols]], 1)
-            v = jnp.concatenate([values[low, :, cols], values[high, :, cols]], 1)
-            out = lax.dot_general(probs[p, h], v, FIRST, preferred_element_type=F32)
-            gq = lax.dot_general(grad_s[p, h], k, FIRST, preferred_element_type=F32) * SCALE
-            for j, both in enumerate((out, gq)):
-                picked = jnp.where(top, both[:, :HS], both[:, HS:]).astype(BF16)
-                results[pl.ds(2 * p, 2), j, :, cols] = picked.reshape(2, CLEN, HS)
-        return carry
-
-    lax.fori_loop(0, groups // 2, answers, 0, unroll=4)
-    answer_copy, answers_arrive, answers_leave = send_to_group(
-        groups, lambda g: results.at[g], answers_in, answer_send, answer_recv
+        cross_copy(c).start()
+        return carry
+
+    lax.fori_loop(0, blocks, send_cross, 0)
+    answer_all(grad_s, keys, SCALE, after)
+    grad_q_to, grad_qs_arrive, grad_qs_leave = send_to_group(
+        groups, lambda g: slot_view(after, g), grad_qs_in, grad_q_send, grad_q_recv
     )
-    start_all(groups, answer_copy)
-    local_answer = pltpu.make_async_copy(results.at[me], answers_in.at[me], local_sem.at[1])
-    local_answer.start()
-
-    def send_near(c, carry):
-        d = blocks - 1 - c
-        to_up[c] = part(c, 2).astype(BF16)
-        sum_up(c).start()
-        to_down[d] = part(d, 1).astype(BF16)
-        sum_down(d).start()
-        return carry
-
-    lax.fori_loop(half, blocks, send_near, 0)
-
-    def send_joined(c, carry):
-        d = blocks - 1 - c
-        mine = part(c, 2)
-        far_up(c).wait_recv()
-        to_up[c] = (mine + from_far[c].astype(F32)).astype(BF16)
-        sum_up(c).start()
-        mine = part(d, 1)
-        far_down(d).wait_recv()
-        to_down[d] = (mine + from_far[d].astype(F32)).astype(BF16)
-        sum_down(d).start()
-        return carry
-
-    lax.fori_loop(0, half, send_joined, 0)
-
-    def keep_own(c, carry):
-        mine = part(c, 0)
+    start_all(groups, grad_q_to)
+    local_grad_q = pltpu.make_async_copy(slot_view(after, me), grad_qs_in.at[me], load_sem.at[0])
+    local_grad_q.start()
+    halves.wait_recv()
+
+    def send_pair(c, carry):
+        mine = own_part(c, pair_slot)
+        cross_copy(c).wait_recv()
+        to_pair[c] = (mine + cross_part(c, 1)).astype(BF16)
+        pair_copy(c).start()
+        mine = own_part(c, 0) + cross_part(c, 0)
         key_acc[c] = mine[:, :width]
         value_acc[c] = mine[:, width:]
         return carry
 
-    lax.fori_loop(0, blocks, keep_own, 0)
-
-    def total(c, arrived):
-        other = arrived[c].astype(F32)
-        return key_acc[c] + other[:, :width], value_acc[c] + other[:, width:]
-
-    def add_first(c, carry):
-        d = blocks - 1 - c
-        sum_up(c).wait_recv()
-        key_acc[c], value_acc[c] = total(c, from_below)
-        sum_down(d).wait_recv()
-        key_acc[d], value_acc[d] = total(d, from_above)
-        return carry
-
-    lax.fori_loop(half, blocks, add_first, 0)
-    local_answer.wait()
-    answers_arrive()
-    answers_leave()
+    lax.fori_loop(0, blocks, send_pair, 0)
+
+    def add_pair(c, carry):
+        pair_copy(c).wait_recv()
+        other = pair_sums[c].astype(F32)
+        grad_e[c, :, :width] = (key_acc[c] + other[:, :width]).astype(BF16)
+        grad_e[c, :, width:] = (value_acc[c] + other[:, width:]).astype(BF16)
+        return carry
+
+    lax.fori_loop(0, blocks, add_pair, 0)
+    local_out.wait()
+    local_grad_q.wait()
+    outs_arrive()
+    grad_qs_arrive()
+    outs_leave()
+    grad_qs_leave()
     stats_leave()
     backs_leave()
 
     def finish_span(t, carry):
         a, b = reads[0, t], reads[1, t]
-        for j, target in enumerate((attended, grad_q)):
-            target[t] = (answers_in[a, j].astype(F32) + answers_in[b, j].astype(F32)).astype(BF16)
+        for target, parts in ((attended, outs_in), (grad_q, grad_qs_in)):
+            target[t] = (parts[a].astype(F32) + parts[b].astype(F32)).astype(BF16)
         return carry
 
     lax.fori_loop(0, spans, finish_span, 0)
-    def emit(c, arrived):
-        low, high = total(c, arrived)
-        grad_e[c, :, :width] = low.astype(BF16)
-        grad_e[c, :, width:] = high.astype(BF16)
-
-    def add_last(c, carry):
-        d = blocks - 1 - c
-        sum_up(c).wait_recv()
-        emit(c, from_below)
-        sum_down(d).wait_recv()
-        emit(d, from_above)
-        return carry
-
-    lax.fori_loop(0, half, add_last, 0)
-
-    for lane in range(3):
+    for lane in range(2):
         all_sent(lane, far, sum_send)
+    for copy in (pieces, firsts, seconds, halves):
+        copy.wait_send()
 
 
 def params(collective_id=None, mib=56):
@@ -588,6 +625,7 @@
 def body(queries, grad_out, encoded, key_weight, value_weight, send_rows, read_slots):
     groups = lax.axis_size(("phase", "dp"))
     ring = lax.axis_size("mp")
+    in_phase = lax.axis_size("dp")
     blocks, _, features = encoded.shape
     width = key_weight.shape[1]
     heads = width // HS
@@ -653,10 +691,11 @@
             pltpu.VMEM((NLEN, width), F32),
             pltpu.VMEM((NLEN, width), F32),
             pltpu.VMEM(slot_shape.shape, BF16),
-            pltpu.VMEM(slot_shape.shape, BF16),
+            pltpu.VMEM((groups, CLEN, width), BF16),
+            pltpu.VMEM((groups, CLEN, width), BF16),
             pltpu.VMEM(encoded.shape, BF16),
             pltpu.VMEM(encoded.shape, BF16),
-            pltpu.VMEM(encoded.shape, BF16),
+            pltpu.VMEM((2 * in_phase, 2, CLEN, width), BF16),
             dma((11,)),
             dma((3,)),
             dma((3, blocks)),
@@ -667,12 +706,16 @@
             dma,
             dma,
             dma,
-            dma((3,)),
-            dma((3, blocks)),
-            dma,
-            dma,
+            dma((2,)),
+            dma((2, blocks)),
+            dma,
+            dma,
+            dma,
+            dma,
+            dma((4,)),
+            dma((4,)),
         ],
-        compiler_params=params(0, 58),
+        compiler_params=params(0, 60),
         name="retro",
     )(rows, reads, query_spans, grad_spans, encoded, key_parts, value_parts)
     return (attended.reshape(queries.shape), grad_q.reshape(queries.shape), grad_e)

time: 173 us -> 162 us (0.936); the launches traced: 173 us -> 160 us
  Pallas kernels: 169 us -> 156 us
    pallas_call x1, Pallas kernels: 169 us -> 156 us  [body(): pl.pallas_call(functools.partial(retro_kernel, groups), out_shape=(pltpu....]
where the time goes in v6:
time: 162 us; the launch traced here: 160 us
  Pallas kernels  156 us (96%)
  local copies, waits for them, and re-layouts  2.91 us (2%)
    pallas_call x1, Pallas kernels, body(): pl.pallas_call(functools.partial(retro_kernel, groups), out_shape=(pltpu....  156 us

profile of v6, /device:TPU:16, one launch (start us, length us, event | category | flops | bytes accessed | tf_op | source)
XLA Modules:
  0.0 160.0 jit_solution(15134565291969558632)
XLA Ops:
  0.6 156.5 %retro.1 = (bf16[8,64,512]{2,1,0:T(8,128)(2,1)S(1)}, bf16[8,64,512]{2,1,0:T(8,128)(2,1)S(1)}, bf16[8,128,1024]{2,1,0:T(8,128)(2,1)S(1)}) custom-call(s32[1,32]{1,0:T(1,128)} %bitcast.15, s32[2,8]{1,0:T(2,128)} %bitcast.14, bf16[8,64,512]{2,1,0:T(8,128)(2,1)} %bitcast.12, bf16[8,64,512]{2,1,0:T(8,128)(2,1)} %bitcast.13, bf16[8,128,1024]{2,1,0:T(8,128)(2,1)} %encoded.1, ...), custom_call_target="tpu_custom_call" | custom-call | tf_op jit(solution)/shard_map/retro/pallas_call | solution.py:652
  157.1 0.8 copy.13
  157.9 0.8 copy.14
  158.7 1.3 copy.15

commit v7 on v6

--- a/solution.py
+++ b/solution.py
@@ -482,13 +482,6 @@
 
         lax.fori_loop(0, groups // 2, one, 0, unroll=4)
 
-    answer_all(probs, values, 1.0, before)
-    out_to, outs_arrive, outs_leave = send_to_group(
-        groups, lambda g: slot_view(before, g), outs_in, answer_send, answer_recv
-    )
-    start_all(groups, out_to)
-    local_out = pltpu.make_async_copy(slot_view(before, me), outs_in.at[me], local_sem.at[1])
-    local_out.start()
     half_lane = lax.broadcasted_iota(jnp.int32, (NLEN, 2 * CLEN), 1) // CLEN
     key_run[...] = jnp.zeros_like(key_run)
     value_run[...] = jnp.zeros_like(value_run)
@@ -563,13 +556,13 @@
         return carry
 
     lax.fori_loop(0, blocks, send_cross, 0)
-    answer_all(grad_s, keys, SCALE, after)
-    grad_q_to, grad_qs_arrive, grad_qs_leave = send_to_group(
-        groups, lambda g: slot_view(after, g), grad_qs_in, grad_q_send, grad_q_recv
+    answer_all(probs, values, 1.0, before)
+    out_to, outs_arrive, outs_leave = send_to_group(
+        groups, lambda g: slot_view(before, g), outs_in, answer_send, answer_recv
     )
-    start_all(groups, grad_q_to)
-    local_grad_q = pltpu.make_async_copy(slot_view(after, me), grad_qs_in.at[me], load_sem.at[0])
-    local_grad_q.start()
+    start_all(groups, out_to)
+    local_out = pltpu.make_async_copy(slot_view(before, me), outs_in.at[me], local_sem.at[1])
+    local_out.start()
     halves.wait_recv()
 
     def send_pair(c, carry):
@@ -582,7 +575,15 @@
         value_acc[c] = mine[:, width:]
         return carry
 
-    lax.fori_loop(0, blocks, send_pair, 0)
+    lax.fori_loop(0, 2, send_pair, 0)
+    answer_all(grad_s, keys, SCALE, after)
+    grad_q_to, grad_qs_arrive, grad_qs_leave = send_to_group(
+        groups, lambda g: slot_view(after, g), grad_qs_in, grad_q_send, grad_q_recv
+    )
+    start_all(groups, grad_q_to)
+    local_grad_q = pltpu.make_async_copy(slot_view(after, me), grad_qs_in.at[me], load_sem.at[0])
+    local_grad_q.start()
+    lax.fori_loop(2, blocks, send_pair, 0)
 
     def add_pair(c, carry):
         pair_copy(c).wait_recv()

time: 162 us -> 159 us (0.981)
  no operation moved by 1% of the time
where the time goes in v7:
time: 159 us
  Pallas kernels  155 us (97%)
  local copies, waits for them, and re-layouts  2.91 us (2%)
    pallas_call x1, Pallas kernels, body(): pl.pallas_call(functools.partial(retro_kernel, groups), out_shape=(pltpu....  155 us

profile of v7, /device:TPU:16, one launch (start us, length us, event | category | flops | bytes accessed | tf_op | source)
XLA Modules:
  0.0 158.5 jit_solution(11032740018553953981)
XLA Ops:
  0.6 155.0 %retro.1 = (bf16[8,64,512]{2,1,0:T(8,128)(2,1)S(1)}, bf16[8,64,512]{2,1,0:T(8,128)(2,1)S(1)}, bf16[8,128,1024]{2,1,0:T(8,128)(2,1)S(1)}) custom-call(s32[1,32]{1,0:T(1,128)} %bitcast.15, s32[2,8]{1,0:T(2,128)} %bitcast.14, bf16[8,64,512]{2,1,0:T(8,128)(2,1)} %bitcast.12, bf16[8,64,512]{2,1,0:T(8,128)(2,1)} %bitcast.13, bf16[8,128,1024]{2,1,0:T(8,128)(2,1)} %encoded.1, ...), custom_call_target="tpu_custom_call" | custom-call | tf_op jit(solution)/shard_map/retro/pallas_call | solution.py:653
  155.6 0.8 copy.13
  156.4 0.8 copy.14
  157.2 1.3 copy.15

commit v8 on v7

--- a/solution.py
+++ b/solution.py
@@ -379,7 +379,7 @@
         groups, lambda g: stats.at[g // 2], fetched, stat_send, stat_recv
     )
     local_stat = pltpu.make_async_copy(stats.at[me // 2], fetched.at[me], local_sem.at[2])
-    together = 4
+    together = 2
     chunks = groups // 2 // together
 
     def score_some(j, carry):

time: 159 us -> 159 us (level)
  no operation moved by 1% of the time
where the time goes in v8:
time: 159 us
  Pallas kernels  155 us (97%)
  local copies, waits for them, and re-layouts  2.91 us (2%)
    pallas_call x1, Pallas kernels, body(): pl.pallas_call(functools.partial(retro_kernel, groups), out_shape=(pltpu....  155 us

profile of v8, /device:TPU:16, one launch (start us, length us, event | category | flops | bytes accessed | tf_op | source)
XLA Modules:
  0.0 158.6 jit_solution(2591324232578744706)
XLA Ops:
  0.6 155.0 %retro.1 = (bf16[8,64,512]{2,1,0:T(8,128)(2,1)S(1)}, bf16[8,64,512]{2,1,0:T(8,128)(2,1)S(1)}, bf16[8,128,1024]{2,1,0:T(8,128)(2,1)S(1)}) custom-call(s32[1,32]{1,0:T(1,128)} %bitcast.15, s32[2,8]{1,0:T(2,128)} %bitcast.14, bf16[8,64,512]{2,1,0:T(8,128)(2,1)} %bitcast.12, bf16[8,64,512]{2,1,0:T(8,128)(2,1)} %bitcast.13, bf16[8,128,1024]{2,1,0:T(8,128)(2,1)} %encoded.1, ...), custom_call_target="tpu_custom_call" | custom-call | tf_op jit(solution)/shard_map/retro/pallas_call | solution.py:653
  155.6 0.8 copy.13
  156.4 0.8 copy.14
  157.2 1.3 copy.15
